TPU v7x, 32 devices: a whole 2x2x4 slice. The times are simulated.
32 devices in a mesh: dp: 8 (over z, x), tensor: 4 (over y, core).
Axes of the slice: x: 2, y: 2, z: 4, core: 2. Of those that a mesh axis runs over, the one named last changes fastest.
Arguments:
- tokens_in: bfloat16 [12288, 768], P('dp'), may hold values from -6 to 6
- cotangent: bfloat16 [12288, 768], P('dp'), may hold values from -6 to 6
- span_mask: int32 [12288], P('dp'), may hold values from 0 to 1, as said below
- lengths: int32 [24], P('dp'), may hold values from 128 to 512, as said below
- step: int32 [1], replicated, may hold values from 1000 to 31999
- warmup: int32 [1], replicated, may hold values from 1000 to 29999
- total: int32 [1], replicated, may hold values from 32000 to 40000
- w_qkv: float32 [768, 3, 768], P(None, None, 'tensor'), may hold values from -0.21875 to 0.21875
- w_out: float32 [768, 768], P(None, 'tensor'), may hold values from -1.25 to 1.25
- w_in: float32 [768, 3072], P(None, 'tensor'), may hold values from -0.21875 to 0.21875
- w_back: float32 [768, 3072], P(None, 'tensor'), may hold values from -0.109375 to 0.109375
- gains: float32 [2, 768], replicated, may hold values from 0.5 to 1.5
- biases: float32 [6, 768], replicated, may hold values from -3 to 3
- bias_in: float32 [3072], replicated, may hold values from -3 to 3
- mom_qkv: float32 [2, 768, 3, 768], P(None, 'dp', None, 'tensor'), as said below
- mom_out: float32 [2, 768, 768], P(None, 'dp', 'tensor'), as said below
- mom_in: float32 [2, 768, 3072], P(None, 'dp', 'tensor'), as said below
- mom_back: float32 [2, 768, 3072], P(None, 'dp', 'tensor'), as said below
- mom_gains: float32 [2, 2, 768], replicated, as said below
- mom_biases: float32 [2, 6, 768], replicated, as said below
- mom_bias_in: float32 [2, 3072], replicated, as said below
Outputs:
- normed_out: bfloat16 [12288, 768], P('dp')
- input_grad: float32 [12288, 768], P('dp')
- change_qkv: float32 [768, 3, 768], P(None, None, 'tensor')
- change_out_proj: float32 [768, 768], P(None, 'tensor')
- change_in_proj: float32 [768, 3072], P(None, 'tensor')
- change_back_proj: float32 [768, 3072], P(None, 'tensor')
- change_gains: float32 [2, 768], replicated
- change_biases: float32 [6, 768], replicated
- change_bias_in: float32 [3072], replicated
- new_mom_qkv: float32 [2, 768, 3, 768], P(None, 'dp', None, 'tensor')
- new_mom_out: float32 [2, 768, 768], P(None, 'dp', 'tensor')
- new_mom_in: float32 [2, 768, 3072], P(None, 'dp', 'tensor')
- new_mom_back: float32 [2, 768, 3072], P(None, 'dp', 'tensor')
- new_mom_gains: float32 [2, 2, 768], replicated
- new_mom_biases: float32 [2, 6, 768], replicated
- new_mom_bias_in: float32 [2, 3072], replicated
Inputs may be any that keep to these rules, and one draw needn't show every extreme that they name: `span_mask`: marked positions lie below their sequence's length and form unions of spans of 1 to 10 positions; each sequence has at most 76 of them, and in every draw each of the 3 sequences of some index of dp has exactly 76. `lengths`: a sequence's real tokens stand at its start, the rest is padding. step < total. warmup < total. `mom_qkv`: index 1 of the leading dimension holds positive second moments. `mom_out`: index 1 of the leading dimension holds positive second moments. `mom_in`: index 1 of the leading dimension holds positive second moments. `mom_back`: index 1 of the leading dimension holds positive second moments. `mom_gains`: index 1 of the leading dimension holds positive second moments. `mom_biases`: index 1 of the leading dimension holds positive second moments. `mom_bias_in`: index 1 of the leading dimension holds positive second moments.
All inputs are finite; a program needn't handle non-finite values.
Results may differ from a plain program's by a relative error of at most 0.017.
The roundings to bfloat16 on the way count: a program that leaves them out, or rounds other values in their place, can miss the bound.
Values sent between devices are 32-bit elements; how exact they have to be, the bound alone decides.
A program may use at most 128 MiB of HBM per device.

v0:
```python
import math

import jax
import jax.numpy as jnp
from jax import lax
from jax.sharding import PartitionSpec as P

HD = 64


NORM_EPS = 1e-12
BETA_ONE = 0.9
BETA_TWO = 0.999
ADAM_EPS = 1e-06
WEIGHT_DECAY = 0.01


def layer_norm(values, gain, shift):
    center = values - jnp.mean(values, axis=-1, keepdims=True)
    spread = jnp.mean(center * center, axis=-1, keepdims=True)
    return center * lax.rsqrt(spread + NORM_EPS) * gain + shift


def exact_gelu(values):
    return jax.nn.gelu(values, approximate=False)


def outer_sum(left, right):
    return jnp.einsum("ta,tb->ab", left, right, preferred_element_type=jnp.float32)


def adam_step(weight, grad, moments, ratio, corr_one, corr_two, decay):
    first = BETA_ONE * moments[0] + (1.0 - BETA_ONE) * grad
    second = BETA_TWO * moments[1] + (1.0 - BETA_TWO) * grad * grad
    update = first / corr_one / (jnp.sqrt(second / corr_two) + ADAM_EPS) + decay * weight
    return (-ratio * update, jnp.stack([first, second]))


def on_device(
    tokens_in,
    cotangent,
    span_mask,
    lengths,
    step,
    warmup,
    total,
    w_qkv,
    w_out,
    w_in,
    w_back,
    gains,
    biases,
    bias_in,
    mom_qkv,
    mom_out,
    mom_in,
    mom_back,
    mom_gains,
    mom_biases,
    mom_bias_in,
):
    row_count, model_width = tokens_in.shape
    seq_count = lengths.shape[0]
    seq_length = row_count // seq_count
    head_cols = w_qkv.shape[2]
    hidden_cols = w_in.shape[1]
    head_size = HD
    local_heads = head_cols // head_size
    query_scale = 1.0 / math.sqrt(head_size)
    tensor_slot = lax.axis_index("tensor")
    bias_query = lax.dynamic_slice_in_dim(biases[0], tensor_slot * head_cols, head_cols)
    bias_value = lax.dynamic_slice_in_dim(biases[1], tensor_slot * head_cols, head_cols)
    bias_hidden = lax.dynamic_slice_in_dim(bias_in, tensor_slot * hidden_cols, hidden_cols)
    qkv_low = w_qkv.astype(jnp.bfloat16).reshape(model_width, 3 * head_cols)
    out_low = w_out.astype(jnp.bfloat16)
    in_low = w_in.astype(jnp.bfloat16)
    down_low = w_back.astype(jnp.bfloat16)
    projected = jnp.dot(tokens_in, qkv_low, preferred_element_type=jnp.float32).reshape(
        row_count, 3, head_cols
    )
    attn_shape = (seq_count, seq_length, local_heads, head_size)
    queries = (
        ((projected[:, 0] + bias_query) * query_scale).astype(jnp.bfloat16).reshape(attn_shape)
    )
    keys = projected[:, 1].astype(jnp.bfloat16).reshape(attn_shape)
    values = (projected[:, 2] + bias_value).astype(jnp.bfloat16).reshape(attn_shape)
    positions = jnp.arange(seq_length, dtype=jnp.int32)
    inside = positions[None, :] < lengths[:, None]
    key_bias = jnp.where(inside, 0.0, -1000000000.0).astype(jnp.float32)

    def score_block():
        raw = jnp.einsum("sqhd,skhd->shqk", queries, keys, preferred_element_type=jnp.float32)
        return raw + key_bias[:, None, None, :]

    scores = score_block()
    peak = jnp.max(scores, axis=-1, keepdims=True)
    log_total = peak + jnp.log(jnp.sum(jnp.exp(scores - peak), axis=-1, keepdims=True))
    probs_low = jnp.exp(scores - log_total).astype(jnp.bfloat16)
    context_low = (
        jnp.einsum("shqk,skhd->sqhd", probs_low, values, preferred_element_type=jnp.float32)
        .reshape(row_count, head_cols)
        .astype(jnp.bfloat16)
    )
    attn_part = jnp.einsum("tc,dc->td", context_low, out_low, preferred_element_type=jnp.float32)
    attn_sum = lax.psum(attn_part, "tensor")
    residual_one = tokens_in.astype(jnp.float32) + attn_sum + biases[2]
    normed = layer_norm(residual_one, gains[0], biases[3])
    normed_low = normed.astype(jnp.bfloat16)
    pre_act = jnp.dot(normed_low, in_low, preferred_element_type=jnp.float32) + bias_hidden
    act_low = exact_gelu(pre_act).astype(jnp.bfloat16)
    down_part = jnp.einsum("tf,df->td", act_low, down_low, preferred_element_type=jnp.float32)
    down_sum = lax.psum(down_part, "tensor")
    residual_two = normed + down_sum + biases[4]
    result, norm_two_back = jax.vjp(layer_norm, residual_two, gains[1], biases[5])
    normed_out = result.astype(jnp.bfloat16)
    live_int = inside.reshape(row_count).astype(jnp.int32) * span_mask
    live = live_int.astype(jnp.float32)
    grad_result = cotangent.astype(jnp.float32) * live[:, None]
    d_res_two, d_gain_two, d_shift_two = norm_two_back(grad_result)
    d_res_two_low = d_res_two.astype(jnp.bfloat16)
    grad_back = outer_sum(d_res_two_low, act_low)
    d_act = jnp.dot(d_res_two_low, down_low, preferred_element_type=jnp.float32)
    _, gelu_back = jax.vjp(exact_gelu, pre_act)
    d_pre = gelu_back(d_act)[0]
    d_pre_low = d_pre.astype(jnp.bfloat16)
    grad_in = outer_sum(normed_low, d_pre_low)
    d_normed_part = jnp.einsum("tf,df->td", d_pre_low, in_low, preferred_element_type=jnp.float32)
    d_normed = lax.psum(d_normed_part, "tensor") + d_res_two
    _, norm_one_back = jax.vjp(layer_norm, residual_one, gains[0], biases[3])
    d_res_one, d_gain_one, d_shift_one = norm_one_back(d_normed)
    d_res_one_low = d_res_one.astype(jnp.bfloat16)
    grad_out_proj = outer_sum(d_res_one_low, context_low)
    d_context = (
        jnp.dot(d_res_one_low, out_low, preferred_element_type=jnp.float32)
        .astype(jnp.bfloat16)
        .reshape(attn_shape)
    )
    probs = jnp.exp(score_block() - log_total)
    probs_again = probs.astype(jnp.bfloat16)
    d_probs = jnp.einsum("sqhd,skhd->shqk", d_context, values, preferred_element_type=jnp.float32)
    d_values = jnp.einsum(
        "shqk,sqhd->skhd", probs_again, d_context, preferred_element_type=jnp.float32
    ).reshape(row_count, head_cols)
    d_scores = (probs * (d_probs - jnp.sum(probs * d_probs, axis=-1, keepdims=True))).astype(
        jnp.bfloat16
    )
    d_queries = (
        jnp.einsum("shqk,skhd->sqhd", d_scores, keys, preferred_element_type=jnp.float32).reshape(
            row_count, head_cols
        )
        * query_scale
    )
    d_keys = jnp.einsum(
        "shqk,sqhd->skhd", d_scores, queries, preferred_element_type=jnp.float32
    ).reshape(row_count, head_cols)
    d_proj_low = (
        jnp.stack([d_queries, d_keys, d_values], axis=1)
        .astype(jnp.bfloat16)
        .reshape(row_count, 3 * head_cols)
    )
    grad_qkv = outer_sum(tokens_in, d_proj_low).reshape(model_width, 3, head_cols)
    d_entry_part = jnp.einsum("tc,dc->td", d_proj_low, qkv_low, preferred_element_type=jnp.float32)
    input_grad = lax.psum(d_entry_part, "tensor") + d_res_one
    first_rank = (tensor_slot == 0).astype(jnp.float32)
    width_zero = jnp.zeros((model_width,), jnp.float32)

    def place_heads(partial_sum):
        return lax.dynamic_update_slice_in_dim(width_zero, partial_sum, tensor_slot * head_cols, 0)

    grad_gains = jnp.stack([d_gain_one, d_gain_two]) * first_rank
    grad_biases = jnp.stack(
        [
            place_heads(jnp.sum(d_queries, axis=0)),
            place_heads(jnp.sum(d_values, axis=0)),
            jnp.sum(d_res_one, axis=0) * first_rank,
            d_shift_one * first_rank,
            jnp.sum(d_res_two, axis=0) * first_rank,
            d_shift_two * first_rank,
        ]
    )
    grad_bias_in = lax.dynamic_update_slice_in_dim(
        jnp.zeros(bias_in.shape, jnp.float32), jnp.sum(d_pre, axis=0), tensor_slot * hidden_cols, 0
    )
    grad_gains, grad_biases, grad_bias_in = lax.psum(
        (grad_gains, grad_biases, grad_bias_in), ("dp", "tensor")
    )
    data_slot = lax.axis_index("dp")
    shard_rows = model_width // lax.axis_size("dp")
    summed = lax.psum((grad_qkv, grad_out_proj, grad_in, grad_back), "dp")
    owned = tuple(
        (
            lax.dynamic_slice_in_dim(whole_sum, data_slot * shard_rows, shard_rows, 0)
            for whole_sum in summed
        )
    )
    clock = step[0].astype(jnp.float32)
    warm = warmup[0].astype(jnp.float32)
    horizon = total[0].astype(jnp.float32)
    ratio = jnp.minimum(clock / warm, (horizon - clock) / (horizon - warm))
    corr_one = 1.0 - jnp.power(BETA_ONE, clock)
    corr_two = 1.0 - jnp.power(BETA_TWO, clock)
    change_rows = []
    fresh_moments = []
    for weight, grad_rows, moment in zip(
        (w_qkv, w_out, w_in, w_back), owned, (mom_qkv, mom_out, mom_in, mom_back)
    ):
        weight_rows = lax.dynamic_slice_in_dim(weight, data_slot * shard_rows, shard_rows, 0)
        row_change, new_moment = adam_step(
            weight_rows, grad_rows, moment, ratio, corr_one, corr_two, WEIGHT_DECAY
        )
        change_rows.append(row_change)
        fresh_moments.append(new_moment)
    change_qkv, change_out_proj, change_in_proj, change_back_proj = (
        lax.all_gather(change_rows[0], "dp", axis=0, tiled=True),
        lax.all_gather(change_rows[1], "dp", axis=0, tiled=True),
        lax.all_gather(change_rows[2], "dp", axis=0, tiled=True),
        lax.all_gather(change_rows[3], "dp", axis=0, tiled=True),
    )
    change_gains, new_mom_gains = adam_step(
        gains, grad_gains, mom_gains, ratio, corr_one, corr_two, 0.0
    )
    change_biases, new_mom_biases = adam_step(
        biases, grad_biases, mom_biases, ratio, corr_one, corr_two, 0.0
    )
    change_bias_in, new_mom_bias_in = adam_step(
        bias_in, grad_bias_in, mom_bias_in, ratio, corr_one, corr_two, 0.0
    )
    return (
        normed_out,
        input_grad,
        change_qkv,
        change_out_proj,
        change_in_proj,
        change_back_proj,
        change_gains,
        change_biases,
        change_bias_in,
        fresh_moments[0],
        fresh_moments[1],
        fresh_moments[2],
        fresh_moments[3],
        new_mom_gains,
        new_mom_biases,
        new_mom_bias_in,
    )


def solution(mesh):
    in_specs = (
        P("dp", None),
        P("dp", None),
        P("dp"),
        P("dp"),
        P(),
        P(),
        P(),
        P(None, None, "tensor"),
        P(None, "tensor"),
        P(None, "tensor"),
        P(None, "tensor"),
        P(),
        P(),
        P(),
        P(None, "dp", None, "tensor"),
        P(None, "dp", "tensor"),
        P(None, "dp", "tensor"),
        P(None, "dp", "tensor"),
        P(),
        P(),
        P(),
    )
    out_specs = (
        P("dp", None),
        P("dp", None),
        P(None, None, "tensor"),
        P(None, "tensor"),
        P(None, "tensor"),
        P(None, "tensor"),
        P(),
        P(),
        P(),
        P(None, "dp", None, "tensor"),
        P(None, "dp", "tensor"),
        P(None, "dp", "tensor"),
        P(None, "dp", "tensor"),
        P(),
        P(),
        P(),
    )
    return jax.shard_map(
        on_device, mesh=mesh, in_specs=in_specs, out_specs=out_specs, check_vma=False
    )
```

profile of v0, /device:TPU:0, one launch (start us, length us, event | category | flops | bytes accessed | tf_op | source)
XLA Modules:
  0.0 939.9 jit_solution(9173336511828967916)
XLA Ops:
  7.2 3.8 fusion.10
  11.1 1.2 fusion.80
  12.6 1.1 convert_element_type.98
  13.8 0.9 squeeze.4
  14.7 1.9 squeeze.5
  16.6 2.9 add_reduce_fusion
  19.6 1.8 exponential_reduce_fusion
  21.8 1.4 copy-done
  23.2 1.7 fusion.12
  25.6 3.0 fusion.45
  28.7 12.0 %all-reduce.10.cloned.1.call-start = ((), (), s32[]{:S(2)}) async-start(), calls=%async_computation.1 | async-start | bytes 9437184 | tf_op jit(solution)/shard_map/psum | solution.py:112
  40.7 0.8 dynamic_slice.35
  41.5 84.0 %all-reduce.8.cloned.1.call-done = f32[1536,768]{1,0:T(8,128)} async-done(((f32[1536,768]{1,0:T(8,128)}), f32[1536,768]{1,0:T(8,128)}) %all-reduce.8.cloned.1.call-update) | async-done | bytes 4718608 | tf_op jit(solution)/shard_map/psum | solution.py:105
  125.6 3.8 fusion.79
  130.1 2.6 copy-done.19
  132.7 14.4 %multiply_convert_fusion.1 = (bf16[1536,768]{1,0:T(8,128)(2,1)S(1)}, f32[1536,768]{1,0:T(8,128)}, f32[1536,768]{1,0:T(8,128)}) fusion(f32[768]{0:T(1024)S(1)} %dynamic_slice.35, f32[768,768]{1,0:T(8,128)S(1)} %copy-done.19, f32[1536,768]{1,0:T(8,128)S(1)} %get-tuple-element.96, f32[768]{0:T(1024)S(1)} %get-tuple-element.125, ...), kind=kOutput, calls=%fused_computation.21 | convolution fusion | flops 1896284160 | bytes 18895872 | tf_op jit(solution)/shard_map/dot_general | solution.py:109
  147.1 1.4 copy-done.39
  148.5 4.3 fusion.24
  153.6 93.7 %all-reduce.10.cloned.1.call-done = f32[1536,768]{1,0:T(8,128)} async-done(((f32[1536,768]{1,0:T(8,128)}), f32[1536,768]{1,0:T(8,128)}) %all-reduce.10.cloned.1.call-update) | async-done | bytes 4718608 | tf_op jit(solution)/shard_map/psum | solution.py:112
  247.2 4.7 fusion.77
  252.6 1.0 copy-done.4
  253.6 2.8 multiply_reduce_fusion.1
  256.5 3.7 fusion.76
  260.2 4.5 fusion.85
  264.7 1.4 copy-done.40
  266.1 4.3 fusion.17
  270.5 6.9 fusion.72
  277.4 6.4 fusion.15
  283.8 81.0 %all-reduce.12.cloned.1.call-done = f32[1536,768]{1,0:T(8,128)} async-done(((f32[1536,768]{1,0:T(8,128)}), f32[1536,768]{1,0:T(8,128)}) %all-reduce.12.cloned.1.call-update) | async-done | bytes 4718608 | tf_op jit(solution)/shard_map/psum | solution.py:128
  364.7 7.5 multiply_reduce_fusion.2
  372.2 3.8 fusion.75
  376.1 2.4 fusion.73
  378.5 1.0 convolution_convert_fusion
  380.0 6.4 fusion.84
  386.4 5.7 multiply_reduce_fusion
  392.1 2.3 multiply_convert_fusion
  394.5 1.6 convolution_bitcast_fusion.2
  396.1 1.6 fusion.83
  398.1 0.8 stack_reshape.7
  399.5 1.0 mul.594
  401.0 0.8 stack_reshape.6
  402.1 4.4 fusion.88
  406.5 2.9 copy.94
  409.5 5.7 convolution_bitcast_fusion
  417.9 1.2 constant_dynamic-slice_fusion.1
  419.2 247.8 %all-reduce.16.cloned.1.call-done = (f32[768,3,192]{2,0,1:T(8,128)}, f32[768,192]{1,0:T(8,128)}, f32[768,768]{1,0:T(8,128)}, f32[768,768]{1,0:T(8,128)}) async-done(((f32[768,3,192]{2,0,1:T(8,128)}, f32[768,192]{1,0:T(8,128)}, f32[768,768]{1,0:T(8,128)}, f32[768,768]{1,0:T(8,128)}), (f32[768,3,192]{2,0,1:T(8,128)}, f32[768,192]{1,0:T(8,128)}, f32[768,768]{1,0:T(8,128)}, ...) | async-done | bytes 7077904 | tf_op jit(solution)/shard_map/psum | solution.py:189
  667.1 1.9 fusion.50
  669.1 2.0 fusion.48
  671.2 2.2 fusion.49
  674.6 87.7 %all-reduce.14.cloned.1.call-done = f32[1536,768]{1,0:T(8,128)} async-done(((f32[1536,768]{1,0:T(8,128)}), f32[1536,768]{1,0:T(8,128)}) %all-reduce.14.cloned.1.call-update) | async-done | bytes 4718608 | tf_op jit(solution)/shard_map/psum | solution.py:163
  762.4 6.5 add_reduce_fusion.1
  769.0 41.3 %all-reduce = (f32[2,768]{1,0:T(2,128)S(1)}, f32[6,768]{1,0:T(8,128)S(1)}, f32[3072]{0:T(1024)S(1)}) all-reduce(f32[2,768]{1,0:T(2,128)S(1)} %maximum_multiply_fusion, f32[6,768]{1,0:T(8,128)S(1)} %stack.89, f32[3072]{0:T(1024)S(1)} %dynamic_update_slice.13), channel_id=1, replica_groups=mesh['dp'=8,'tensor'=4] {'dp','tensor'}, use_global_device_ids=true, to_apply=%region_21.22 | all-reduce | flops 9216 | bytes 73728 | tf_op jit(solution)/shard_map/psum | solution.py:184
  814.1 1.0 fusion.58
  815.1 33.2 %all_gather.13 = f32[768,192]{1,0:T(8,128)S(1)} all-gather(f32[96,192]{1,0:T(8,128)S(1)} %get-tuple-element.114), channel_id=1, replica_groups=mesh['dp'=8,'tensor'=4] {'dp'}, dimensions={0}, use_global_device_ids=true | all-gather | bytes 663552 | tf_op jit(solution)/shard_map/all_gather | solution.py:215
  848.3 1.1 copy.100
  849.4 0.7 pad_maximum_fusion.3
  850.0 0.9 pad_maximum_fusion
  850.9 0.9 pad_maximum_fusion.2
  851.8 0.9 pad_maximum_fusion.1
  852.6 2.9 copy.99
  855.5 19.2 %all-gather.6.cloned.1.call-done = f32[768,768]{1,0:T(8,128)} async-done(((f32[96,768]{1,0:T(8,128)}), f32[768,768]{1,0:T(8,128)}) %all-gather.6.cloned.1.call-update) | async-done | bytes 2359312 | tf_op jit(solution)/shard_map/all_gather | solution.py:216
  874.7 53.4 %all-gather.8.cloned.1.call-done = f32[768,768]{1,0:T(8,128)} async-done(((f32[96,768]{1,0:T(8,128)}), f32[768,768]{1,0:T(8,128)}) %all-gather.8.cloned.1.call-update) | async-done | bytes 2359312 | tf_op jit(solution)/shard_map/all_gather | solution.py:217
  928.1 3.4 copy.176
  931.5 1.4 copy.177
  (173 shorter events, 11.3 us)
Async XLA Ops:
  7.2 118.4 %all-reduce.8.cloned.1.call-start = ((), (), s32[]{:S(2)}) async-start(), calls=%async_computation | async-start | bytes 9437184 | tf_op jit(solution)/shard_map/psum | solution.py:105
  11.0 1.3 copy-start.38
  11.0 1.3 copy-start.15
  12.6 6.9 copy-start.17
  19.6 3.6 copy-start
  21.4 3.5 copy-start.10
  23.2 1.8 copy-start.5
  23.2 2.4 copy-start.8
  28.7 12.9 %copy-start.25 = (f32[2,768]{1,0:T(2,128)S(1)}, f32[2,768]{1,0:T(2,128)}, u32[]{:S(2)}) copy-start(f32[2,768]{1,0:T(2,128)} %param.32) | copy-start | bytes 18436
  28.7 218.5 %all-reduce.10.cloned.1.call-start = ((), (), s32[]{:S(2)}) async-start(), calls=%async_computation.1 | async-start | bytes 9437184 | tf_op jit(solution)/shard_map/psum | solution.py:112
  129.4 17.8 %copy-start.1 = (f32[1536,768]{1,0:T(8,128)}, f32[1536,768]{1,0:T(8,128)S(1)}, u32[]{:S(2)}) copy-start(f32[1536,768]{1,0:T(8,128)S(1)} %get-tuple-element.96) | copy-start | bytes 14155780
  129.4 3.4 copy-start.19
  132.7 15.8 %copy-start.21 = (f32[768,768]{1,0:T(8,128)S(1)}, f32[768,768]{1,0:T(8,128)}, u32[]{:S(2)}) copy-start(f32[768,768]{1,0:T(8,128)} %param.31) | copy-start | bytes 7077892
  147.1 1.4 copy-start.39
  152.9 0.7 copy-start.36
  152.9 211.9 %all-reduce.12.cloned.1.call-start = ((), (), s32[]{:S(2)}) async-start(), calls=%async_computation.2 | async-start | bytes 9437184 | tf_op jit(solution)/shard_map/psum | solution.py:128
  252.0 1.7 copy-start.4
  253.6 6.5 slice-start.3
  253.6 6.5 slice-start.5
  256.5 3.7 copy-start.22
  256.5 3.7 slice-start.4
  256.5 3.7 slice-start.6
  260.2 4.6 copy-start.3
  260.2 5.9 copy-start.20
  264.7 1.4 copy-start.40
  270.4 396.7 %all-reduce.16.cloned.1.call-start = ((), (), s32[]{:S(2)}) async-start(), calls=%async_computation.7 | async-start | bytes 15728640 | tf_op jit(solution)/shard_map/psum | solution.py:189
  270.5 6.9 copy-start.41
  376.1 2.4 copy-start.2
  380.0 6.4 copy-start.6
  380.0 6.4 copy-start.11
  380.0 12.1 %slice-start = ((s8[9437184]{0:T(1024)(128)(4,1)}), s8[4194304]{0:T(1024)(128)(4,1)S(1)}, s32[]{:S(2)}) async-start(s8[9437184]{0:T(1024)(128)(4,1)} %bitcast.159), calls=%async_computation.8 | async-start | bytes 8388608
  380.0 12.1 %slice-start.1 = ((s8[9437184]{0:T(1024)(128)(4,1)}), s8[4194304]{0:T(1024)(128)(4,1)S(1)}, s32[]{:S(2)}) async-start(s8[9437184]{0:T(1024)(128)(4,1)} %bitcast.159), calls=%async_computation.9 | async-start | bytes 8388608
  386.4 5.7 slice-start.2
  392.1 2.3 copy-start.18
  394.5 1.6 copy-start.7
  409.4 352.9 %all-reduce.14.cloned.1.call-start = ((), (), s32[]{:S(2)}) async-start(), calls=%async_computation.3 | async-start | bytes 9437184 | tf_op jit(solution)/shard_map/psum | solution.py:163
  415.2 251.9 %copy-start.12 = (f32[2,96,3,192]{3,1,2,0:T(8,128)S(1)}, f32[2,96,3,192]{3,1,2,0:T(8,128)}, u32[]{:S(2)}) copy-start(f32[2,96,3,192]{3,1,2,0:T(8,128)} %param.35) | copy-start | bytes 1327108
  415.2 253.9 %copy-start.13 = (f32[2,96,768]{2,1,0:T(8,128)S(1)}, f32[2,96,768]{2,1,0:T(8,128)}, u32[]{:S(2)}) copy-start(f32[2,96,768]{2,1,0:T(8,128)} %param.37) | copy-start | bytes 1769476
  415.2 255.9 %copy-start.24 = (f32[2,3072]{1,0:T(2,128)S(1)}, f32[2,3072]{1,0:T(2,128)}, u32[]{:S(2)}) copy-start(f32[2,3072]{1,0:T(2,128)} %param.41) | copy-start | bytes 73732
  415.2 258.4 %copy-start.23 = (f32[2,6,768]{2,0,1:T(2,128)S(1)}, f32[2,6,768]{2,0,1:T(2,128)}, u32[]{:S(2)}) copy-start(f32[2,6,768]{2,0,1:T(2,128)} %param.40) | copy-start | bytes 110596
  415.2 258.4 %copy-start.28 = (f32[768]{0:T(1024)S(1)}, f32[768]{0:T(1024)}, u32[]{:S(2)}) copy-start(f32[768]{0:T(1024)} %get-tuple-element.66) | copy-start | bytes 9220
  415.3 258.4 %copy-start.29 = (f32[768]{0:T(1024)S(1)}, f32[768]{0:T(1024)}, u32[]{:S(2)}) copy-start(f32[768]{0:T(1024)} %get-tuple-element.69) | copy-start | bytes 9220
  415.3 258.4 %copy-start.37 = (f32[768]{0:T(1024)S(1)}, f32[768]{0:T(1024)}, u32[]{:S(2)}) copy-start(f32[768]{0:T(1024)} %get-tuple-element.140) | copy-start | bytes 9220
  415.3 258.7 %copy-start.30 = (f32[768]{0:T(1024)S(1)}, f32[768]{0:T(1024)}, u32[]{:S(2)}) copy-start(f32[768]{0:T(1024)} %get-tuple-element.64) | copy-start | bytes 9220
  415.3 258.7 %copy-start.32 = (f32[768]{0:T(1024)S(1)}, f32[768]{0:T(1024)}, u32[]{:S(2)}) copy-start(f32[768]{0:T(1024)} %get-tuple-element.68) | copy-start | bytes 9220
  415.3 258.8 %copy-start.31 = (f32[768]{0:T(1024)S(1)}, f32[768]{0:T(1024)}, u32[]{:S(2)}) copy-start(f32[768]{0:T(1024)} %get-tuple-element.98) | copy-start | bytes 9220
  415.3 258.8 %copy-start.34 = (f32[3,64]{1,0:T(4,128)S(1)}, f32[3,64]{1,0:T(4,128)}, u32[]{:S(2)}) copy-start(f32[3,64]{1,0:T(4,128)} %get-tuple-element.138) | copy-start | bytes 2308
  415.3 258.9 %copy-start.35 = (f32[3,64]{1,0:T(4,128)S(1)}, f32[3,64]{1,0:T(4,128)}, u32[]{:S(2)}) copy-start(f32[3,64]{1,0:T(4,128)} %get-tuple-element.136) | copy-start | bytes 2308
  415.3 437.3 %all-gather.4.cloned.1.call-start = ((), (), s32[]{:S(2)}) async-start(), calls=%async_computation.4 | async-start | bytes 2654208 | tf_op jit(solution)/shard_map/all_gather | solution.py:214
  669.0 205.7 %all-gather.6.cloned.1.call-start = ((), (), s32[]{:S(2)}) async-start(), calls=%async_computation.5 | async-start | bytes 2654208 | tf_op jit(solution)/shard_map/all_gather | solution.py:216
  671.1 257.0 %all-gather.8.cloned.1.call-start = ((), (), s32[]{:S(2)}) async-start(), calls=%async_computation.6 | async-start | bytes 2654208 | tf_op jit(solution)/shard_map/all_gather | solution.py:217
  674.6 135.7 %copy-start.16 = (f32[6,768]{1,0:T(8,128)S(1)}, f32[6,768]{1,0:T(8,128)}, u32[]{:S(2)}) copy-start(f32[6,768]{1,0:T(8,128)} %param.33) | copy-start | bytes 55300
  674.6 137.0 %copy-start.26 = (f32[2,768]{1,0:T(2,128)S(1)}, f32[2,768]{1,0:T(2,128)}, u32[]{:S(2)}) copy-start(f32[2,768]{1,0:T(2,128)} %param.32) | copy-start | bytes 18436
  674.6 137.0 %copy-start.33 = (f32[2,2,768]{2,1,0:T(2,128)S(1)}, f32[2,2,768]{2,1,0:T(2,128)}, u32[]{:S(2)}) copy-start(f32[2,2,768]{2,1,0:T(2,128)} %param.39) | copy-start | bytes 36868
  674.6 138.2 %copy-start.27 = (f32[3072]{0:T(1024)S(1)}, f32[3072]{0:T(1024)}, u32[]{:S(2)}) copy-start(f32[3072]{0:T(1024)} %param.34) | copy-start | bytes 36868
  674.6 139.5 %copy-start.14 = (f32[2,96,192]{2,1,0:T(8,128)S(1)}, f32[2,96,192]{2,1,0:T(8,128)}, u32[]{:S(2)}) copy-start(f32[2,96,192]{2,1,0:T(8,128)} %param.36) | copy-start | bytes 442372
  928.1 3.4 copy-start.9
Sparse Core Ops, SparseCore 0:
  28.8 96.7 all-reduce.7
  153.0 94.1 all-reduce.9
  270.5 94.1 all-reduce.11
  409.6 257.4 all-reduce.15
  669.3 93.0 all-reduce.13
  765.0 52.6 all-gather.3
  820.4 54.2 all-gather.5
  877.5 50.5 all-gather.7
where the time goes:
time: 948 us; the launch traced here: 940 us
  waiting for transfers between devices  667 us (70%)
  matrix products  80.9 us (9%)
  blocking collectives  74.5 us (8%)
  other arithmetic  52.6 us (6%)
  local copies, waits for them, and re-layouts  34.9 us (4%)
  between operations  17.7 us (2%)
  starting transfers between devices  12.3 us (1%)
    psum x1, waiting for transfers between devices, on_device(): summed = lax.psum((grad_qkv, grad_out_proj, grad_in, grad_back), 'dp')  248 us
    psum x1, waiting for transfers between devices, on_device(): down_sum = lax.psum(down_part, 'tensor')  93.7 us
    psum x1, waiting for transfers between devices, on_device(): input_grad = lax.psum(d_entry_part, 'tensor') + d_res_one  87.7 us
    psum x1, waiting for transfers between devices, on_device(): attn_sum = lax.psum(attn_part, 'tensor')  84 us
    psum x1, waiting for transfers between devices, on_device(): d_normed = lax.psum(d_normed_part, 'tensor') + d_res_two  81 us
    all_gather x1, waiting for transfers between devices, on_device(): lax.all_gather(change_rows[3], 'dp', axis=0, tiled=True)  53.4 us
    psum x1, blocking collectives, on_device(): lax.psum((grad_gains, grad_biases, grad_bias_in), ('dp', 'tensor'))  41.3 us
    all_gather x1, blocking collectives, on_device(): lax.all_gather(change_rows[1], 'dp', axis=0, tiled=True)  33.2 us
  transfers between devices with their start and end apart: 8, of which 7 were waited for; matrix products, arithmetic and copies ran while one was open for 5% of the time, Pallas kernels for 0%

commit v1 on v0

--- a/solution.py
+++ b/solution.py
@@ -6,6 +6,7 @@
 from jax.sharding import PartitionSpec as P
 
 HD = 64
+SPAN_ROWS = 80
 
 
 NORM_EPS = 1e-12
@@ -111,31 +112,62 @@
     down_part = jnp.einsum("tf,df->td", act_low, down_low, preferred_element_type=jnp.float32)
     down_sum = lax.psum(down_part, "tensor")
     residual_two = normed + down_sum + biases[4]
-    result, norm_two_back = jax.vjp(layer_norm, residual_two, gains[1], biases[5])
+    live = (inside.astype(jnp.int32) * span_mask.reshape(seq_count, seq_length)) > 0
+    upto = (positions[:, None] <= positions[None, :]).astype(jnp.float32)
+    rank = jnp.dot(live.astype(jnp.float32), upto).astype(jnp.int32) - 1
+    slots = jnp.arange(SPAN_ROWS, dtype=jnp.int32)
+    pick = (live[:, None, :] & (rank[:, None, :] == slots[None, :, None])).astype(jnp.float32)
+    pick_low = pick.astype(jnp.bfloat16)
+
+    def rows_of(values):
+        width = values.shape[-1]
+        return jnp.einsum(
+            "srt,std->srd",
+            pick,
+            values.reshape(seq_count, seq_length, width),
+            precision=lax.Precision.HIGHEST,
+        ).reshape(seq_count * SPAN_ROWS, width)
+
+    def low_rows_of(values):
+        width = values.shape[-1]
+        return jnp.einsum(
+            "srt,std->srd",
+            pick_low,
+            values.reshape(seq_count, seq_length, width),
+            preferred_element_type=jnp.bfloat16,
+        ).reshape(seq_count * SPAN_ROWS, width)
+
+    result = layer_norm(residual_two, gains[1], biases[5])
     normed_out = result.astype(jnp.bfloat16)
-    live_int = inside.reshape(row_count).astype(jnp.int32) * span_mask
-    live = live_int.astype(jnp.float32)
-    grad_result = cotangent.astype(jnp.float32) * live[:, None]
+    residual_one_rows = rows_of(residual_one)
+    residual_two_rows = rows_of(residual_two)
+    grad_result = low_rows_of(cotangent).astype(jnp.float32)
+    _, norm_two_back = jax.vjp(layer_norm, residual_two_rows, gains[1], biases[5])
     d_res_two, d_gain_two, d_shift_two = norm_two_back(grad_result)
     d_res_two_low = d_res_two.astype(jnp.bfloat16)
-    grad_back = outer_sum(d_res_two_low, act_low)
+    normed_low_rows = low_rows_of(normed_low)
+    pre_rows = jnp.dot(normed_low_rows, in_low, preferred_element_type=jnp.float32) + bias_hidden
+    act_rows, gelu_back = jax.vjp(exact_gelu, pre_rows)
+    grad_back = outer_sum(d_res_two_low, act_rows.astype(jnp.bfloat16))
     d_act = jnp.dot(d_res_two_low, down_low, preferred_element_type=jnp.float32)
-    _, gelu_back = jax.vjp(exact_gelu, pre_act)
     d_pre = gelu_back(d_act)[0]
     d_pre_low = d_pre.astype(jnp.bfloat16)
-    grad_in = outer_sum(normed_low, d_pre_low)
+    grad_in = outer_sum(normed_low_rows, d_pre_low)
     d_normed_part = jnp.einsum("tf,df->td", d_pre_low, in_low, preferred_element_type=jnp.float32)
     d_normed = lax.psum(d_normed_part, "tensor") + d_res_two
-    _, norm_one_back = jax.vjp(layer_norm, residual_one, gains[0], biases[3])
+    _, norm_one_back = jax.vjp(layer_norm, residual_one_rows, gains[0], biases[3])
     d_res_one, d_gain_one, d_shift_one = norm_one_back(d_normed)
     d_res_one_low = d_res_one.astype(jnp.bfloat16)
-    grad_out_proj = outer_sum(d_res_one_low, context_low)
+    grad_out_proj = outer_sum(d_res_one_low, low_rows_of(context_low))
+    row_shape = (seq_count, SPAN_ROWS, local_heads, head_size)
     d_context = (
         jnp.dot(d_res_one_low, out_low, preferred_element_type=jnp.float32)
         .astype(jnp.bfloat16)
-        .reshape(attn_shape)
-    )
-    probs = jnp.exp(score_block() - log_total)
+        .reshape(row_shape)
+    )
+    query_rows = low_rows_of(queries.reshape(row_count, head_cols)).reshape(row_shape)
+    raw = jnp.einsum("sqhd,skhd->shqk", query_rows, keys, preferred_element_type=jnp.float32)
+    probs = jax.nn.softmax(raw + key_bias[:, None, None, :], axis=-1)
     probs_again = probs.astype(jnp.bfloat16)
     d_probs = jnp.einsum("sqhd,skhd->shqk", d_context, values, preferred_element_type=jnp.float32)
     d_values = jnp.einsum(
@@ -146,21 +178,31 @@
     )
     d_queries = (
         jnp.einsum("shqk,skhd->sqhd", d_scores, keys, preferred_element_type=jnp.float32).reshape(
-            row_count, head_cols
+            seq_count * SPAN_ROWS, head_cols
         )
         * query_scale
     )
     d_keys = jnp.einsum(
-        "shqk,sqhd->skhd", d_scores, queries, preferred_element_type=jnp.float32
+        "shqk,sqhd->skhd", d_scores, query_rows, preferred_element_type=jnp.float32
     ).reshape(row_count, head_cols)
+
+    def spread(row_values):
+        width = row_values.shape[-1]
+        return jnp.einsum(
+            "srt,srd->std",
+            pick,
+            row_values.reshape(seq_count, SPAN_ROWS, width),
+            precision=lax.Precision.HIGHEST,
+        ).reshape(row_count, width)
+
     d_proj_low = (
-        jnp.stack([d_queries, d_keys, d_values], axis=1)
+        jnp.stack([spread(d_queries), d_keys, d_values], axis=1)
         .astype(jnp.bfloat16)
         .reshape(row_count, 3 * head_cols)
     )
     grad_qkv = outer_sum(tokens_in, d_proj_low).reshape(model_width, 3, head_cols)
     d_entry_part = jnp.einsum("tc,dc->td", d_proj_low, qkv_low, preferred_element_type=jnp.float32)
-    input_grad = lax.psum(d_entry_part, "tensor") + d_res_one
+    input_grad = lax.psum(d_entry_part, "tensor") + spread(d_res_one)
     first_rank = (tensor_slot == 0).astype(jnp.float32)
     width_zero = jnp.zeros((model_width,), jnp.float32)
 
@@ -186,12 +228,9 @@
     )
     data_slot = lax.axis_index("dp")
     shard_rows = model_width // lax.axis_size("dp")
-    summed = lax.psum((grad_qkv, grad_out_proj, grad_in, grad_back), "dp")
     owned = tuple(
-        (
-            lax.dynamic_slice_in_dim(whole_sum, data_slot * shard_rows, shard_rows, 0)
-            for whole_sum in summed
-        )
+        lax.psum_scatter(part, "dp", scatter_dimension=0, tiled=True)
+        for part in (grad_qkv, grad_out_proj, grad_in, grad_back)
     )
     clock = step[0].astype(jnp.float32)
     warm = warmup[0].astype(jnp.float32)

time: 948 us -> 903 us (0.953)
  waiting for transfers between devices: 667 us -> 611 us
  local copies, waits for them, and re-layouts: 34.9 us -> 48.5 us
  starting transfers between devices: 12.3 us -> 1.56 us
    psum x2 -> x1, waiting for transfers between devices: 336 us -> 60.6 us  [on_device(): input_grad = lax.psum(d_entry_part, 'tensor') + spread(d_res_one)]
    reduce_scatter x0 -> x4, waiting for transfers between devices: none -> 194 us  [on_device(): lax.psum_scatter(part, 'dp', scatter_dimension=0, tiled=True)]
    psum x1, waiting for transfers between devices: 81 us -> 34 us  [on_device(): d_normed = lax.psum(d_normed_part, 'tensor') + d_res_two]
    all_gather x1, waiting for transfers between devices: 0.01 us -> 46 us  [on_device(): lax.all_gather(change_rows[0], 'dp', axis=0, tiled=True)]
    all_gather x1, waiting for transfers between devices: 19.2 us -> 50.6 us  [on_device(): lax.all_gather(change_rows[2], 'dp', axis=0, tiled=True)]
    psum x1, waiting for transfers between devices: 93.7 us -> 78 us  [on_device(): down_sum = lax.psum(down_part, 'tensor')]
    dot_general x1, matrix products: 4.32 us -> 17.8 us  [on_device(): jnp.einsum('tf,df->td', act_low, down_low, preferred_element_type=jnp.flo...]
    psum x1, starting transfers between devices: 12 us -> 0.51 us  [on_device(): down_sum = lax.psum(down_part, 'tensor')]
  transfers between devices with their start and end apart: 8 -> 11, of which waited for: 7 -> 11; matrix products, arithmetic and copies ran while one was open for 5% -> 8% of each run, Pallas kernels for 0% -> 0%
where the time goes in v1:
time: 903 us; the launch traced here: 894 us
  waiting for transfers between devices  611 us (68%)
  matrix products  86.9 us (10%)
  blocking collectives  72.4 us (8%)
  other arithmetic  56.1 us (6%)
  local copies, waits for them, and re-layouts  48.5 us (5%)
  between operations  17.5 us (2%)
    reduce_scatter x4, waiting for transfers between devices, on_device(): lax.psum_scatter(part, 'dp', scatter_dimension=0, tiled=True)  194 us
    psum x1, waiting for transfers between devices, on_device(): attn_sum = lax.psum(attn_part, 'tensor')  94.2 us
    psum x1, waiting for transfers between devices, on_device(): down_sum = lax.psum(down_part, 'tensor')  78 us
    psum x1, waiting for transfers between devices, on_device(): input_grad = lax.psum(d_entry_part, 'tensor') + spread(d_res_one)  60.6 us
    all_gather x1, waiting for transfers between devices, on_device(): lax.all_gather(change_rows[3], 'dp', axis=0, tiled=True)  53.1 us
    all_gather x1, waiting for transfers between devices, on_device(): lax.all_gather(change_rows[2], 'dp', axis=0, tiled=True)  50.6 us
    all_gather x1, waiting for transfers between devices, on_device(): lax.all_gather(change_rows[0], 'dp', axis=0, tiled=True)  46 us
    psum x1, blocking collectives, on_device(): lax.psum((grad_gains, grad_biases, grad_bias_in), ('dp', 'tensor'))  40.3 us
  transfers between devices with their start and end apart: 11, of which 11 were waited for; matrix products, arithmetic and copies ran while one was open for 8% of the time, Pallas kernels for 0%

profile of v1, /device:TPU:0, one launch (start us, length us, event | category | flops | bytes accessed | tf_op | source)
XLA Modules:
  0.0 894.0 jit_solution(5073173420024962855)
XLA Ops:
  7.2 3.9 fusion.15
  13.9 2.1 convert_element_type.129
  16.0 1.7 squeeze.7
  18.3 1.8 fusion.168
  20.9 1.8 multiply_convert_fusion
  22.7 2.8 add_reduce_fusion
  25.6 1.8 exponential_reduce_fusion
  27.3 1.8 copy-done.3
  29.8 2.8 squeeze.6
  32.7 1.8 add_convert_fusion.1
  34.5 5.7 fusion.20
  41.2 3.0 fusion.96
  46.9 94.2 %all-reduce.6.cloned.1.call-done = f32[1536,768]{1,0:T(8,128)} async-done(((f32[1536,768]{1,0:T(8,128)}), f32[1536,768]{1,0:T(8,128)}) %all-reduce.6.cloned.1.call-update) | async-done | bytes 4718608 | tf_op jit(solution)/shard_map/psum | solution.py:106
  141.1 3.8 fusion.167
  145.7 1.4 copy-done.2
  147.1 2.1 fusion.14
  149.2 17.8 %fusion.18 = f32[1536,768]{1,0:T(8,128)} fusion(bf16[1536,768]{1,0:T(8,128)(2,1)} %fusion.14, f32[768]{0:T(1024)} %dynamic_slice.23, f32[768,768]{1,0:T(8,128)} %param.31, f32[768,768]{1,0:T(8,128)} %param.30), kind=kOutput, calls=%fused_computation.39 | convolution fusion | flops 3702915072 | bytes 11799552 | tf_op jit(solution)/shard_map/tf,df->td/dot_general | solution.py:112
  167.2 1.8 squeeze.8
  170.6 2.0 fusion.35
  172.6 3.1 fusion.175
  175.7 4.6 fusion.173
  183.3 78.0 %all-reduce.8.cloned.1.call-done = f32[1536,768]{1,0:T(8,128)} async-done(((f32[1536,768]{1,0:T(8,128)}), f32[1536,768]{1,0:T(8,128)}) %all-reduce.8.cloned.1.call-update) | async-done | bytes 4718608 | tf_op jit(solution)/shard_map/psum | solution.py:113
  261.3 5.3 fusion.166
  266.7 2.2 copy-done.4
  268.9 2.1 fusion.174
  271.0 2.0 multiply_reduce_fusion.8
  273.2 1.4 fusion.100
  274.8 1.4 fusion.25
  276.3 4.8 fusion.180
  283.1 34.0 %all-reduce.10.cloned.1.call-done = f32[240,768]{1,0:T(8,128)} async-done(((f32[240,768]{1,0:T(8,128)}), f32[240,768]{1,0:T(8,128)}) %all-reduce.10.cloned.1.call-update) | async-done | bytes 737296 | tf_op jit(solution)/shard_map/psum | solution.py:157
  317.0 2.2 fusion.163
  320.9 1.5 convolution_convert_fusion.1
  323.2 2.6 fusion.179
  327.9 1.7 fusion.178
  330.9 1.8 copy.94
  332.7 1.5 stack_reshape.10
  334.2 1.6 fusion.49
  336.3 1.5 stack_reshape.9
  337.9 1.4 maximum_convert_fusion
  339.3 4.4 fusion.181
  343.7 3.0 copy.97
  346.8 1.9 fusion.89
  348.8 4.6 fusion.62
  355.3 6.1 convolution_bitcast_fusion
  365.1 50.8 %reduce-scatter.5.cloned.1.call-done = f32[96,3,192]{2,0,1:T(8,128)} async-done(((f32[768,3,192]{2,0,1:T(8,128)}), f32[96,3,192]{2,0,1:T(8,128)}) %reduce-scatter.5.cloned.1.call-update) | async-done | bytes 221200 | tf_op jit(solution)/shard_map/reduce_scatter | solution.py:232
  415.9 2.2 fusion.104
  418.2 69.9 %reduce-scatter.9.cloned.1.call-done = f32[96,768]{1,0:T(8,128)} async-done(((f32[768,768]{1,0:T(8,128)}), f32[96,768]{1,0:T(8,128)}) %reduce-scatter.9.cloned.1.call-update) | async-done | bytes 294928 | tf_op jit(solution)/shard_map/reduce_scatter | solution.py:232
  488.0 2.2 fusion.105
  492.5 3.0 multiply_reduce_fusion
  495.6 4.2 add_convert_fusion
  499.8 59.7 %reduce-scatter.11.cloned.1.call-done = f32[96,768]{1,0:T(8,128)} async-done(((f32[768,768]{1,0:T(8,128)}), f32[96,768]{1,0:T(8,128)}) %reduce-scatter.11.cloned.1.call-update) | async-done | bytes 294928 | tf_op jit(solution)/shard_map/reduce_scatter | solution.py:232
  559.6 2.0 fusion.106
  562.6 40.3 %all-reduce = (f32[2,768]{1,0:T(2,128)S(1)}, f32[6,768]{1,0:T(8,128)S(1)}, f32[3072]{0:T(1024)S(1)}) all-reduce(f32[2,768]{1,0:T(2,128)S(1)} %maximum_multiply_fusion, f32[6,768]{1,0:T(8,128)S(1)} %stack.88, f32[3072]{0:T(1024)S(1)} %dynamic_update_slice.13), channel_id=1, replica_groups=mesh['dp'=8,'tensor'=4] {'dp','tensor'}, use_global_device_ids=true, to_apply=%region_27.28 | all-reduce | flops 9216 | bytes 73728 | tf_op jit(solution)/shard_map/psum | solution.py:226
  606.8 4.3 fusion.47
  611.1 13.9 %reduce-scatter.7.cloned.1.call-done = f32[96,192]{1,0:T(8,128)} async-done(((f32[768,192]{1,0:T(8,128)}), f32[96,192]{1,0:T(8,128)}) %reduce-scatter.7.cloned.1.call-update) | async-done | bytes 73744 | tf_op jit(solution)/shard_map/reduce_scatter | solution.py:232
  626.1 32.1 %all_gather.13 = f32[768,192]{1,0:T(8,128)S(1)} all-gather(f32[96,192]{1,0:T(8,128)S(1)} %get-tuple-element.107), channel_id=1, replica_groups=mesh['dp'=8,'tensor'=4] {'dp'}, dimensions={0}, use_global_device_ids=true | all-gather | bytes 663552 | tf_op jit(solution)/shard_map/all_gather | solution.py:254
  660.0 60.6 %all-reduce.12.cloned.1.call-done = f32[1536,768]{1,0:T(8,128)} async-done(((f32[1536,768]{1,0:T(8,128)}), f32[1536,768]{1,0:T(8,128)}) %all-reduce.12.cloned.1.call-update) | async-done | bytes 4718608 | tf_op jit(solution)/shard_map/psum | solution.py:205
  720.6 6.6 bitcast_add_fusion
  729.7 46.0 %all-gather.4.cloned.1.call-done = f32[768,3,192]{2,0,1:T(8,128)} async-done(((f32[96,3,192]{2,0,1:T(8,128)}), f32[768,3,192]{2,0,1:T(8,128)}) %all-gather.4.cloned.1.call-update) | async-done | bytes 1769488 | tf_op jit(solution)/shard_map/all_gather | solution.py:253
  775.7 2.9 copy.102
  778.6 50.6 %all-gather.6.cloned.1.call-done = f32[768,768]{1,0:T(8,128)} async-done(((f32[96,768]{1,0:T(8,128)}), f32[768,768]{1,0:T(8,128)}) %all-gather.6.cloned.1.call-update) | async-done | bytes 2359312 | tf_op jit(solution)/shard_map/all_gather | solution.py:255
  829.2 53.1 %all-gather.8.cloned.1.call-done = f32[768,768]{1,0:T(8,128)} async-done(((f32[96,768]{1,0:T(8,128)}), f32[768,768]{1,0:T(8,128)}) %all-gather.8.cloned.1.call-update) | async-done | bytes 2359312 | tf_op jit(solution)/shard_map/all_gather | solution.py:256
  882.2 3.4 copy.181
  885.6 1.4 copy.182
  (237 shorter events, 38.7 us)
Async XLA Ops:
  7.2 263.8 %copy-start = (bf16[1536,768]{1,0:T(8,128)(2,1)S(1)}, bf16[1536,768]{1,0:T(8,128)(2,1)}, u32[]{:S(2)}) copy-start(bf16[1536,768]{1,0:T(8,128)(2,1)} %param.22) | copy-start | bytes 7077892
  7.2 133.9 %all-reduce.6.cloned.1.call-start = ((), (), s32[]{:S(2)}) async-start(), calls=%async_computation.4 | async-start | bytes 9437184 | tf_op jit(solution)/shard_map/psum | solution.py:106
  11.2 2.7 copy-start.63
  25.5 3.6 copy-start.3
  25.6 7.0 copy-start.60
  34.4 5.7 copy-start.15
  34.5 6.7 copy-start.19
  44.2 217.1 %all-reduce.8.cloned.1.call-start = ((), (), s32[]{:S(2)}) async-start(), calls=%async_computation.5 | async-start | bytes 9437184 | tf_op jit(solution)/shard_map/psum | solution.py:113
  144.9 2.2 copy-start.2
  144.9 2.2 copy-start.39
  167.0 150.0 %all-reduce.10.cloned.1.call-start = ((), (), s32[]{:S(2)}) async-start(), calls=%async_computation.6 | async-start | bytes 1474560 | tf_op jit(solution)/shard_map/psum | solution.py:157
  172.6 9.3 %copy-start.26 = (bf16[3,80,192]{1,2,0:T(8,128)(2,1)}, bf16[3,80,192]{1,2,0:T(8,128)(2,1)S(1)}, u32[]{:S(2)}) copy-start(bf16[3,80,192]{1,2,0:T(8,128)(2,1)S(1)} %fusion.35) | copy-start | bytes 276484
  175.7 5.7 copy-start.10
  175.7 6.2 copy-start.8
  175.7 6.2 copy-start.55
  180.2 81.1 %copy-start.31 = (f32[1536]{0:T(1024)S(1)}, f32[1536]{0:T(1024)}, u32[]{:S(2)}) copy-start(f32[1536]{0:T(1024)} %copy-done.30) | copy-start | bytes 18436
  180.3 81.1 %copy-start.35 = (f32[1536]{0:T(1024)S(1)}, f32[1536]{0:T(1024)}, u32[]{:S(2)}) copy-start(f32[1536]{0:T(1024)} %copy-done.34) | copy-start | bytes 18436
  180.3 81.1 %copy-start.40 = (f32[768]{0:T(1024)S(1)}, f32[768]{0:T(1024)}, u32[]{:S(2)}) copy-start(f32[768]{0:T(1024)} %get-tuple-element.118) | copy-start | bytes 9220
  180.3 81.0 %copy-start.57 = (f32[768]{0:T(1024)S(1)}, f32[768]{0:T(1024)}, u32[]{:S(2)}) copy-start(f32[768]{0:T(1024)} %get-tuple-element.119) | copy-start | bytes 9220
  266.7 2.2 copy-start.4
  273.2 7.9 copy-start.45
  273.2 7.9 copy-start.47
  274.6 6.4 copy-start.49
  276.3 4.8 copy-start.17
  276.3 4.8 copy-start.9
  282.5 133.4 %reduce-scatter.5.cloned.1.call-start = ((), (), s32[]{:S(2)}) async-start(), calls=%async_computation.8 | async-start | bytes 2654208 | tf_op jit(solution)/shard_map/reduce_scatter | solution.py:232
  320.9 4.9 copy-start.11
  323.2 2.6 copy-start.16
  323.2 2.6 copy-start.29
  330.9 8.4 copy-start.21
  343.7 3.1 copy-start.24
  346.7 141.3 %reduce-scatter.9.cloned.1.call-start = ((), (), s32[]{:S(2)}) async-start(), calls=%async_computation.11 | async-start | bytes 2654208 | tf_op jit(solution)/shard_map/reduce_scatter | solution.py:232
  348.8 4.7 copy-start.14
  348.8 210.8 %reduce-scatter.11.cloned.1.call-start = ((), (), s32[]{:S(2)}) async-start(), calls=%async_computation.13 | async-start | bytes 2654208 | tf_op jit(solution)/shard_map/reduce_scatter | solution.py:232
  353.4 271.6 %reduce-scatter.7.cloned.1.call-start = ((), (), s32[]{:S(2)}) async-start(), calls=%async_computation.10 | async-start | bytes 884736 | tf_op jit(solution)/shard_map/reduce_scatter | solution.py:232
  355.0 365.5 %all-reduce.12.cloned.1.call-start = ((), (), s32[]{:S(2)}) async-start(), calls=%async_computation.7 | async-start | bytes 9437184 | tf_op jit(solution)/shard_map/psum | solution.py:205
  361.4 130.0 %copy-start.38 = (f32[2,6,768]{2,0,1:T(2,128)S(1)}, f32[2,6,768]{2,0,1:T(2,128)}, u32[]{:S(2)}) copy-start(f32[2,6,768]{2,0,1:T(2,128)} %param.40) | copy-start | bytes 110596
  361.4 130.0 %copy-start.42 = (f32[2,3072]{1,0:T(2,128)S(1)}, f32[2,3072]{1,0:T(2,128)}, u32[]{:S(2)}) copy-start(f32[2,3072]{1,0:T(2,128)} %param.41) | copy-start | bytes 73732
  361.4 130.7 %copy-start.7 = (f32[3,80,768]{2,1,0:T(8,128)S(1)}, f32[3,80,768]{2,1,0:T(8,128)}, u32[]{:S(2)}) copy-start(f32[3,80,768]{2,1,0:T(8,128)} %get-tuple-element.137) | copy-start | bytes 2211844
  361.4 130.7 %copy-start.46 = (f32[3,80]{1,0:T(4,128)S(1)}, f32[3,80]{1,0:T(4,128)}, u32[]{:S(2)}) copy-start(f32[3,80]{1,0:T(4,128)} %copy-done.45) | copy-start | bytes 2884
  361.4 130.7 %copy-start.48 = (f32[3,80]{1,0:T(4,128)S(1)}, f32[3,80]{1,0:T(4,128)}, u32[]{:S(2)}) copy-start(f32[3,80]{1,0:T(4,128)} %copy-done.47) | copy-start | bytes 2884
  361.4 130.7 %copy-start.50 = (f32[3,80]{1,0:T(4,128)S(1)}, f32[3,80]{1,0:T(4,128)}, u32[]{:S(2)}) copy-start(f32[3,80]{1,0:T(4,128)} %copy-done.49) | copy-start | bytes 2884
  361.5 131.0 %copy-start.41 = (f32[1536]{0:T(1024)S(1)}, f32[1536]{0:T(1024)}, u32[]{:S(2)}) copy-start(f32[1536]{0:T(1024)} %get-tuple-element.88) | copy-start | bytes 18436
  361.5 414.2 %all-gather.4.cloned.1.call-start = ((), (), s32[]{:S(2)}) async-start(), calls=%async_computation.9 | async-start | bytes 2654208 | tf_op jit(solution)/shard_map/all_gather | solution.py:253
  418.1 77.4 %copy-start.51 = (f32[768]{0:T(1024)S(1)}, f32[768]{0:T(1024)}, u32[]{:S(2)}) copy-start(f32[768]{0:T(1024)} %get-tuple-element.120) | copy-start | bytes 9220
  418.1 411.1 %all-gather.6.cloned.1.call-start = ((), (), s32[]{:S(2)}) async-start(), calls=%async_computation.12 | async-start | bytes 2654208 | tf_op jit(solution)/shard_map/all_gather | solution.py:255
  490.2 392.0 %all-gather.8.cloned.1.call-start = ((), (), s32[]{:S(2)}) async-start(), calls=%async_computation.14 | async-start | bytes 2654208 | tf_op jit(solution)/shard_map/all_gather | solution.py:256
  495.5 64.1 %copy-start.28 = (f32[2,96,768]{2,1,0:T(8,128)S(1)}, f32[2,96,768]{2,1,0:T(8,128)}, u32[]{:S(2)}) copy-start(f32[2,96,768]{2,1,0:T(8,128)} %param.38) | copy-start | bytes 1769476
  495.5 66.1 %copy-start.56 = (f32[768]{0:T(1024)S(1)}, f32[768]{0:T(1024)}, u32[]{:S(2)}) copy-start(f32[768]{0:T(1024)} %get-tuple-element.70) | copy-start | bytes 9220
  495.5 66.2 %copy-start.59 = (f32[768]{0:T(1024)S(1)}, f32[768]{0:T(1024)}, u32[]{:S(2)}) copy-start(f32[768]{0:T(1024)} %get-tuple-element.146) | copy-start | bytes 9220
  495.5 66.5 %copy-start.52 = (f32[768]{0:T(1024)S(1)}, f32[768]{0:T(1024)}, u32[]{:S(2)}) copy-start(f32[768]{0:T(1024)} %get-tuple-element.66) | copy-start | bytes 9220
  495.5 66.5 %copy-start.62 = (f32[3,64]{1,0:T(4,128)S(1)}, f32[3,64]{1,0:T(4,128)}, u32[]{:S(2)}) copy-start(f32[3,64]{1,0:T(4,128)} %get-tuple-element.142) | copy-start | bytes 2308
  495.5 66.5 %copy-start.61 = (f32[3,64]{1,0:T(4,128)S(1)}, f32[3,64]{1,0:T(4,128)}, u32[]{:S(2)}) copy-start(f32[3,64]{1,0:T(4,128)} %get-tuple-element.144) | copy-start | bytes 2308
  495.6 66.6 %copy-start.54 = (f32[768]{0:T(1024)S(1)}, f32[768]{0:T(1024)}, u32[]{:S(2)}) copy-start(f32[768]{0:T(1024)} %get-tuple-element.85) | copy-start | bytes 9220
  495.6 66.6 %copy-start.53 = (f32[768]{0:T(1024)S(1)}, f32[768]{0:T(1024)}, u32[]{:S(2)}) copy-start(f32[768]{0:T(1024)} %get-tuple-element.71) | copy-start | bytes 9220
  495.6 107.4 %copy-start.33 = (f32[6,768]{1,0:T(8,128)S(1)}, f32[6,768]{1,0:T(8,128)}, u32[]{:S(2)}) copy-start(f32[6,768]{1,0:T(8,128)} %param.33) | copy-start | bytes 55300
  495.6 108.7 %copy-start.43 = (f32[2,768]{1,0:T(2,128)S(1)}, f32[2,768]{1,0:T(2,128)}, u32[]{:S(2)}) copy-start(f32[2,768]{1,0:T(2,128)} %param.32) | copy-start | bytes 18436
  495.6 108.7 %copy-start.58 = (f32[2,2,768]{2,1,0:T(2,128)S(1)}, f32[2,2,768]{2,1,0:T(2,128)}, u32[]{:S(2)}) copy-start(f32[2,2,768]{2,1,0:T(2,128)} %param.39) | copy-start | bytes 36868
  495.6 109.9 %copy-start.36 = (f32[1,3072]{1,0:T(1,128)S(1)}, f32[1,3072]{1,0:T(1,128)}, u32[]{:S(2)}) copy-start(f32[1,3072]{1,0:T(1,128)} %get-tuple-element.113) | copy-start | bytes 36868
  495.6 109.9 %copy-start.37 = (f32[1,3072]{1,0:T(1,128)S(1)}, f32[1,3072]{1,0:T(1,128)}, u32[]{:S(2)}) copy-start(f32[1,3072]{1,0:T(1,128)} %get-tuple-element.114) | copy-start | bytes 36868
  495.6 109.9 %copy-start.44 = (f32[3072]{0:T(1024)S(1)}, f32[3072]{0:T(1024)}, u32[]{:S(2)}) copy-start(f32[3072]{0:T(1024)} %param.34) | copy-start | bytes 36868
  660.0 67.2 %copy-start.25 = (f32[1,96,3,192]{3,1,2,0:T(8,128)S(1)}, f32[1,96,3,192]{3,1,2,0:T(8,128)}, u32[]{:S(2)}) copy-start(f32[1,96,3,192]{3,1,2,0:T(8,128)} %get-tuple-element.103) | copy-start | bytes 663556
  882.2 3.4 copy-start.20
  882.2 4.8 copy-start.1
  (11 other events, 18.2 us)
Sparse Core Ops, SparseCore 0:
  44.3 96.7 all-reduce.5
  167.1 94.1 all-reduce.7
  282.6 34.3 all-reduce.9
  346.9 69.0 reduce-scatter.4
  419.8 68.1 reduce-scatter.8
  491.4 68.1 reduce-scatter.10
  563.5 61.5 reduce-scatter.6
  627.5 93.0 all-reduce.11
  723.6 52.0 all-gather.3
  778.5 50.5 all-gather.5
  831.6 50.5 all-gather.7

commit v2 on v1

--- a/solution.py
+++ b/solution.py
@@ -1,15 +1,351 @@
+import functools
 import math
 
 import jax
 import jax.numpy as jnp
 from jax import lax
+from jax.experimental import pallas as pl
+from jax.experimental.pallas import tpu as pltpu
 from jax.sharding import PartitionSpec as P
 
 HD = 64
 SPAN_ROWS = 80
-
-
 NORM_EPS = 1e-12
+MESH = pl.DeviceIdType.MESH
+F32 = jnp.float32
+LOW = jnp.bfloat16
+
+
+def dot(left, right, left_dim, right_dim):
+    return lax.dot_general(
+        left, right, (((left_dim,), (right_dim,)), ((), ())), preferred_element_type=F32
+    )
+
+
+def normalize(rows):
+    center = rows - jnp.mean(rows, axis=-1, keepdims=True)
+    scale = lax.rsqrt(jnp.mean(center * center, axis=-1, keepdims=True) + NORM_EPS)
+    return center * scale, scale
+
+
+def norm_back(grad, gain, unit, scale):
+    weighted = grad * gain
+    return scale * (
+        weighted
+        - jnp.mean(weighted, axis=-1, keepdims=True)
+        - unit * jnp.mean(weighted * unit, axis=-1, keepdims=True)
+    )
+
+
+def row_sum(rows):
+    return jnp.sum(rows, axis=0, keepdims=True)
+
+
+class Peers:
+    def __init__(self):
+        self.d = lax.axis_index("dp")
+        self.t = lax.axis_index("tensor")
+        self.b = lax.rem(self.d, 2)
+        self.c = lax.rem(self.t, 2)
+        self.p = lax.div(self.t, 2)
+        self.u = lax.div(self.d, 2)
+        self.core = (self.d, self.t + 1 - 2 * self.c)
+        self.y = (self.d, lax.rem(self.t + 2, 4))
+        self.x = (self.d + 1 - 2 * self.b, self.t)
+
+
+def send(src, dst, sems, k, peer):
+    copy = pltpu.make_async_remote_copy(
+        src_ref=src, dst_ref=dst, send_sem=sems.at[0, k], recv_sem=sems.at[1, k],
+        device_id=peer, device_id_type=MESH,
+    )
+    copy.start()
+    return copy
+
+
+def local(src, dst, sem):
+    copy = pltpu.make_async_copy(src, dst, sem)
+    copy.start()
+    return copy
+
+
+def greet(peers):
+    barrier = pltpu.get_barrier_semaphore()
+    for peer in peers:
+        pl.semaphore_signal(barrier, inc=1, device_id=peer, device_id_type=MESH)
+    pl.semaphore_wait(barrier, len(peers))
+
+
+def gelu_parts(pre):
+    cdf = 0.5 * (1.0 + lax.erf(pre * (1.0 / math.sqrt(2.0))))
+    pdf = jnp.exp(-0.5 * pre * pre) * (1.0 / math.sqrt(2.0 * math.pi))
+    return pre * cdf, cdf + pre * pdf
+
+
+def k1_kernel(
+    lens, mask, gains, biases, bias_in, x_h, cot_h, wqkv_h, wout_h, win_h, wback_h,
+    gattn, gin, gback, dproj, q_o, k_o, v_o, pick_o, dres1_o, wp_out, vec,
+    x, cot, wqkv, wout, win, wback, wql, wol, wil, wbl,
+    pm, xm, cotm, qm, ctxm, ctxp, ap, apc, unit1, rs1, normed, nlow, act, gp, part, rc1, h1, ry1,
+    part2, rc2, h2, ry2, full2, full, dres2, d2w, d2x, nxw, nxx, dplow, dctx, hw,
+    lsem, rsem,
+):
+    seqs, rows = 3, SPAN_ROWS
+    count = x_h.shape[0]
+    length = count // seqs
+    total = seqs * rows
+    half = total // 2
+    heads = q_o.shape[1]
+    n_heads = heads // HD
+    width = x_h.shape[1]
+    me = Peers()
+
+    loads = [
+        local(x_h, x.at[pl.ds(0, count)], lsem.at[0]),
+        local(wqkv_h, wqkv, lsem.at[1]),
+        local(wout_h, wout, lsem.at[2]),
+        local(win_h, win, lsem.at[3]),
+        local(wback_h, wback, lsem.at[4]),
+        local(cot_h, cot, lsem.at[5]),
+    ]
+    greet((me.core, me.y, me.x))
+
+    loads[2].wait()
+    out_half = pl.ds(pl.multiple_of(me.b * (heads // 2), 8), heads // 2)
+    wo_y = send(wout.at[out_half], wp_out.at[out_half], rsem, 0, me.y)
+    loads[1].wait()
+    wql[...] = wqkv[...].astype(LOW)
+    wol[...] = wout[...].astype(LOW)
+
+    def pick_bias(row, k=heads):
+        out = jnp.zeros((1, k), F32)
+        for slot in range(4):
+            piece = biases[row:row + 1, slot * k:(slot + 1) * k]
+            out = jnp.where(me.t == slot, piece, out)
+        return out
+
+    bias_q, bias_v = pick_bias(0), pick_bias(1)
+    hidden = win.shape[1]
+    lanes = 128
+    bias_h = jnp.concatenate(
+        [bias_in[pl.ds(me.t * (hidden // lanes) + j, 1), :] for j in range(hidden // lanes)], axis=1
+    )
+    upto = (
+        lax.broadcasted_iota(jnp.int32, (length, length), 0)
+        <= lax.broadcasted_iota(jnp.int32, (length, length), 1)
+    ).astype(F32).astype(LOW)
+    position = lax.broadcasted_iota(jnp.int32, (1, length), 1)
+    slot_of = lax.broadcasted_iota(jnp.int32, (rows, length), 0).astype(F32)
+    scale = 1.0 / math.sqrt(HD)
+    loads[0].wait()
+
+    def project(s, _):
+        at = pl.ds(pl.multiple_of(s * length, length), length)
+        xs = x[at, :]
+        q = ((dot(xs, wql[0:heads], 1, 1) + bias_q) * scale).astype(LOW)
+        k = dot(xs, wql[heads:2 * heads], 1, 1).astype(LOW)
+        v = (dot(xs, wql[2 * heads:3 * heads], 1, 1) + bias_v).astype(LOW)
+        q_o[at, :] = q
+        k_o[at, :] = k
+        v_o[at, :] = v
+        parts = length // lanes
+        marks = jnp.concatenate([mask[pl.ds(s * parts + j, 1), :] for j in range(parts)], axis=1)
+        inside = position < lens[s]
+        live = jnp.where(inside, marks, 0).astype(F32)
+        rank = dot(jnp.broadcast_to(live, (8, length)).astype(LOW), upto, 1, 0)[0:1] - 1.0
+        pick = jnp.where((rank == slot_of) & (live > 0.0), 1.0, 0.0).astype(LOW)
+        pick_o[s] = pick
+        here = pl.ds(pl.multiple_of(s * rows, rows), rows)
+        xm[here, :] = dot(pick, xs, 1, 0)
+        qrow = dot(pick, q, 1, 0).astype(LOW)
+        qm[here, :] = qrow
+        key_bias = jnp.where(inside, 0.0, -1000000000.0)
+        pieces = []
+        for h in range(n_heads):
+            col = slice(h * HD, (h + 1) * HD)
+            scores = dot(qrow[:, col], k[:, col], 1, 1) + key_bias
+            e = jnp.exp(scores - jnp.max(scores, axis=-1, keepdims=True))
+            prob = e / jnp.sum(e, axis=-1, keepdims=True)
+            pm[s * n_heads + h] = prob
+            pieces.append(dot(prob.astype(LOW), v[:, col], 1, 0))
+        ctxm[here, :] = jnp.concatenate(pieces, axis=1).astype(LOW).astype(F32)
+        return 0
+
+    lax.fori_loop(0, seqs, project, 0)
+    ctx_y = send(ctxm, ctxp, rsem, 1, me.y)
+    wo_y.wait()
+    wo_x = send(wp_out.at[out_half], wp_out.at[out_half], rsem, 2, me.x)
+    part1 = dot(ctxm[...].astype(LOW), wol[...], 1, 0)
+    for load in loads[3:5]:
+        load.wait()
+    wil[...] = win[...].astype(LOW)
+    wbl[...] = wback[...].astype(LOW)
+    loads[5].wait()
+    for s in range(seqs):
+        cotm[s * rows:(s + 1) * rows, :] = dot(pick_o[s], cot[s * length:(s + 1) * length, :], 1, 0)
+    wo_x.wait()
+    ctx_y.wait()
+    ap[...] = part1 + dot(ctxp[...].astype(LOW), wp_out[...].astype(LOW), 1, 0)
+    ap_c = send(ap, apc, rsem, 3, me.core)
+    ap_c.wait()
+    unit, inv = normalize(xm[...] + (ap[...] + apc[...]) + biases[2:3, :])
+    unit1[...] = unit
+    rs1[...] = inv
+    normed[...] = unit * gains[0:1, :] + biases[3:4, :]
+    nlow[...] = normed[...].astype(LOW)
+    nxw[...] = nlow[...].astype(F32)
+    mine = pl.ds(pl.multiple_of(me.c * half, 8), half)
+    other = pl.ds(pl.multiple_of((1 - me.c) * half, 8), half)
+    nx_x = send(nxw.at[mine], nxx.at[mine], rsem, 5, me.x)
+    for j in range(0, hidden, 256):
+        col = slice(j, j + 256)
+        a, g = gelu_parts(dot(nlow[...], wil[:, col], 1, 0) + bias_h[:, col])
+        act[:, col] = a.astype(LOW)
+        gp[:, col] = g
+    part[...] = dot(act[...], wbl[...], 1, 1)
+
+    def all_reduce(src, rc, hs, ry, dst, base, fill):
+        first = send(src.at[other], rc, rsem, base, me.core)
+        first.wait()
+        hs[...] = src[mine, :] + rc[...]
+        second = send(hs, ry, rsem, base + 1, me.y)
+        fill()
+        second.wait()
+        dst[mine, :] = hs[...] + ry[...]
+        third = send(dst.at[mine], dst.at[mine], rsem, base + 2, me.core)
+        third.wait()
+
+    relay = []
+
+    def fill_one():
+        nx_x.wait()
+        relay.append(send(nxx.at[mine], nxx.at[mine], rsem, 6, me.core))
+
+    all_reduce(part, rc1, h1, ry1, full, 7, fill_one)
+    relay[0].wait()
+    unit, inv = normalize(normed[...] + full[...] + biases[4:5, :])
+    grad = cotm[...]
+    d_two = norm_back(grad, gains[1:2, :], unit, inv)
+    dres2[...] = d_two
+    vec[...] = jnp.zeros(vec.shape, F32)
+    vec[1:2, :] = row_sum(grad * unit)
+    vec[5:6, :] = row_sum(d_two)
+    vec[6:7, :] = row_sum(grad)
+    d2w[...] = d_two.astype(LOW).astype(F32)
+    d2_x = send(d2w.at[mine], d2x.at[mine], rsem, 10, me.x)
+    d2low = d2w[...].astype(LOW)
+    for j in range(0, hidden, 256):
+        col = slice(j, j + 256)
+        d_pre = dot(d2low, wbl[:, col], 1, 0) * gp[:, col]
+        vec[8:9, col] = row_sum(d_pre)
+        dplow[0:total, col] = d_pre.astype(LOW)
+    part2[...] = dot(dplow[0:total, :], wil[...], 1, 1)
+
+    def fill_two():
+        for j in range(0, hidden, 256):
+            col = slice(j, j + 256)
+            gin[:, col] = dot(nlow[...], dplow[0:total, col], 0, 0)
+            gback[:, col] = dot(d2low, act[:, col], 0, 0)
+        d2_x.wait()
+        relay.append(send(d2x.at[mine], d2x.at[mine], rsem, 11, me.core))
+
+    all_reduce(part2, rc2, h2, ry2, full2, 12, fill_two)
+    d_normed = full2[...] + dres2[...]
+    unit = unit1[...]
+    d_one = norm_back(d_normed, gains[0:1, :], unit, rs1[...])
+    dres1_o[...] = d_one
+    vec[0:1, :] = row_sum(d_normed * unit)
+    vec[3:4, :] = row_sum(d_one)
+    vec[4:5, :] = row_sum(d_normed)
+    d1low = d_one.astype(LOW)
+    x[count:count + total, :] = d1low
+    dctx[...] = dot(d1low, wol[...], 1, 1).astype(LOW)
+    relay[1].wait()
+    nlx = nxx[...].astype(LOW)
+    dlx = d2x[...].astype(LOW)
+    for j in range(0, hidden, 256):
+        col = slice(j, j + 256)
+        a, g = gelu_parts(dot(nlx, wil[:, col], 1, 0) + bias_h[:, col])
+        d_pre = (dot(dlx, wbl[:, col], 1, 0) * g).astype(LOW)
+        gin[:, col] += dot(nlx, d_pre, 0, 0)
+        gback[:, col] += dot(dlx, a.astype(LOW), 0, 0)
+
+    def attend(s, carry):
+        dq_sum, dv_sum = carry
+        at = pl.ds(pl.multiple_of(s * length, length), length)
+        here = pl.ds(pl.multiple_of(s * rows, rows), rows)
+        q, k, v, dc = qm[here, :], k_o[at, :], v_o[at, :], dctx[here, :]
+        dqs, dks, dvs = [], [], []
+        for h in range(n_heads):
+            col = slice(h * HD, (h + 1) * HD)
+            prob = pm[s * n_heads + h]
+            d_prob = dot(dc[:, col], v[:, col], 1, 1)
+            dvs.append(dot(prob.astype(LOW), dc[:, col], 0, 0))
+            ds = prob * (d_prob - jnp.sum(prob * d_prob, axis=-1, keepdims=True))
+            ds = ds.astype(LOW)
+            dqs.append(dot(ds, k[:, col], 1, 0) * scale)
+            dks.append(dot(ds, q[:, col], 0, 0))
+        dq = jnp.concatenate(dqs, axis=1)
+        dv = jnp.concatenate(dvs, axis=1)
+        spread = dot(pick_o[s], dq.astype(LOW), 0, 0).astype(LOW)
+        dproj[at, 0:3 * heads] = jnp.concatenate(
+            [spread, jnp.concatenate(dks, axis=1).astype(LOW), dv.astype(LOW)], axis=1
+        )
+        dproj[at, 3 * heads:] = jnp.zeros((length, heads), LOW)
+        return dq_sum + row_sum(dq), dv_sum + row_sum(dv)
+
+    zero = jnp.zeros((1, heads), F32)
+    dq_sum, dv_sum = lax.fori_loop(0, seqs, attend, (zero, zero))
+    dproj[count:count + total, 0:3 * heads] = jnp.zeros((total, 3 * heads), LOW)
+    dproj[count:count + total, 3 * heads:] = ctxm[...].astype(LOW)
+    vec[2:3, :] = jnp.concatenate([dq_sum, dv_sum, jnp.zeros((1, width - 2 * heads), F32)], axis=1)
+    for j in range(0, width, 256):
+        col = slice(j, j + 256)
+        gattn[:, col] = dot(x[...], dproj[:, col], 0, 0)
+
+
+def k1_call(x, cot, mask, lens, wqkv, wout, win, wback, gains, biases, bias_in):
+    count, width = x.shape
+    seqs = lens.shape[0]
+    heads = wout.shape[0]
+    hidden = win.shape[1]
+    length = count // seqs
+    total = seqs * SPAN_ROWS
+    half = total // 2
+    any_ = pl.BlockSpec(memory_space=pl.ANY)
+    vm = pl.BlockSpec(memory_space=pltpu.VMEM)
+    sm = pl.BlockSpec(memory_space=pltpu.SMEM)
+    sds = jax.ShapeDtypeStruct
+    out_shape = (
+        sds((width, width), F32), sds((width, hidden), F32), sds((width, hidden), F32),
+        sds((count + total, width), LOW),
+        sds((count, heads), LOW), sds((count, heads), LOW), sds((count, heads), LOW),
+        sds((seqs, SPAN_ROWS, length), LOW), sds((total, width), F32),
+        sds((heads, width), F32), sds((16, width), F32),
+    )
+    V = pltpu.VMEM
+    wide = lambda r, t=F32: V((r, width), t)
+    scratch = [
+        wide(count + total, LOW), wide(count, LOW), wide(3 * heads), wide(heads), V((width, hidden), F32),
+        V((width, hidden), F32), wide(3 * heads, LOW), wide(heads, LOW), V((width, hidden), LOW), V((width, hidden), LOW),
+        V((seqs * (heads // HD), SPAN_ROWS, length), F32), wide(total), wide(total), V((total, heads), LOW),
+        V((total, heads), F32), V((total, heads), F32), wide(total), wide(total), wide(total), V((total, 1), F32),
+        wide(total), wide(total, LOW), V((total, hidden), LOW), V((total, hidden), F32), wide(total), wide(half), wide(half), wide(half),
+        wide(total), wide(half), wide(half), wide(half), wide(total), wide(total), wide(total), wide(total), wide(total), wide(total), wide(total),
+        V((total, hidden), LOW), V((total, heads), LOW), V((8, 128), F32),
+        pltpu.SemaphoreType.DMA((6,)), pltpu.SemaphoreType.DMA((2, 16)),
+    ]
+    return pl.pallas_call(
+        k1_kernel, out_shape=out_shape,
+        in_specs=[sm, vm, vm, vm, vm] + [any_] * 6,
+        out_specs=(vm,) * len(out_shape),
+        scratch_shapes=scratch,
+        compiler_params=pltpu.CompilerParams(
+            collective_id=1, has_side_effects=True, vmem_limit_bytes=60 * 2**20
+        ),
+    )(lens, mask, gains, biases, bias_in, x, cot, wqkv, wout, win, wback)
+
+
 BETA_ONE = 0.9
 BETA_TWO = 0.999
 ADAM_EPS = 1e-06
@@ -139,52 +475,15 @@
 
     result = layer_norm(residual_two, gains[1], biases[5])
     normed_out = result.astype(jnp.bfloat16)
-    residual_one_rows = rows_of(residual_one)
-    residual_two_rows = rows_of(residual_two)
-    grad_result = low_rows_of(cotangent).astype(jnp.float32)
-    _, norm_two_back = jax.vjp(layer_norm, residual_two_rows, gains[1], biases[5])
-    d_res_two, d_gain_two, d_shift_two = norm_two_back(grad_result)
-    d_res_two_low = d_res_two.astype(jnp.bfloat16)
-    normed_low_rows = low_rows_of(normed_low)
-    pre_rows = jnp.dot(normed_low_rows, in_low, preferred_element_type=jnp.float32) + bias_hidden
-    act_rows, gelu_back = jax.vjp(exact_gelu, pre_rows)
-    grad_back = outer_sum(d_res_two_low, act_rows.astype(jnp.bfloat16))
-    d_act = jnp.dot(d_res_two_low, down_low, preferred_element_type=jnp.float32)
-    d_pre = gelu_back(d_act)[0]
-    d_pre_low = d_pre.astype(jnp.bfloat16)
-    grad_in = outer_sum(normed_low_rows, d_pre_low)
-    d_normed_part = jnp.einsum("tf,df->td", d_pre_low, in_low, preferred_element_type=jnp.float32)
-    d_normed = lax.psum(d_normed_part, "tensor") + d_res_two
-    _, norm_one_back = jax.vjp(layer_norm, residual_one_rows, gains[0], biases[3])
-    d_res_one, d_gain_one, d_shift_one = norm_one_back(d_normed)
-    d_res_one_low = d_res_one.astype(jnp.bfloat16)
-    grad_out_proj = outer_sum(d_res_one_low, low_rows_of(context_low))
-    row_shape = (seq_count, SPAN_ROWS, local_heads, head_size)
-    d_context = (
-        jnp.dot(d_res_one_low, out_low, preferred_element_type=jnp.float32)
-        .astype(jnp.bfloat16)
-        .reshape(row_shape)
-    )
-    query_rows = low_rows_of(queries.reshape(row_count, head_cols)).reshape(row_shape)
-    raw = jnp.einsum("sqhd,skhd->shqk", query_rows, keys, preferred_element_type=jnp.float32)
-    probs = jax.nn.softmax(raw + key_bias[:, None, None, :], axis=-1)
-    probs_again = probs.astype(jnp.bfloat16)
-    d_probs = jnp.einsum("sqhd,skhd->shqk", d_context, values, preferred_element_type=jnp.float32)
-    d_values = jnp.einsum(
-        "shqk,sqhd->skhd", probs_again, d_context, preferred_element_type=jnp.float32
-    ).reshape(row_count, head_cols)
-    d_scores = (probs * (d_probs - jnp.sum(probs * d_probs, axis=-1, keepdims=True))).astype(
-        jnp.bfloat16
-    )
-    d_queries = (
-        jnp.einsum("shqk,skhd->sqhd", d_scores, keys, preferred_element_type=jnp.float32).reshape(
-            seq_count * SPAN_ROWS, head_cols
-        )
-        * query_scale
-    )
-    d_keys = jnp.einsum(
-        "shqk,sqhd->skhd", d_scores, query_rows, preferred_element_type=jnp.float32
-    ).reshape(row_count, head_cols)
+    wqkv_t = jnp.transpose(w_qkv, (1, 2, 0)).reshape(3 * head_cols, model_width)
+    (
+        grad_attn, grad_in, grad_back, d_proj, _, _, _, _, d_res_one, wp_out, vec
+    ) = k1_call(
+        tokens_in, cotangent, span_mask.reshape(-1, 128), lengths, wqkv_t, w_out.T, w_in, w_back,
+        gains, biases, bias_in.reshape(-1, 128)
+    )
+    grad_qkv = grad_attn[:, :3 * head_cols].reshape(model_width, 3, head_cols)
+    grad_out_proj = grad_attn[:, 3 * head_cols:]
 
     def spread(row_values):
         width = row_values.shape[-1]
@@ -195,13 +494,7 @@
             precision=lax.Precision.HIGHEST,
         ).reshape(row_count, width)
 
-    d_proj_low = (
-        jnp.stack([spread(d_queries), d_keys, d_values], axis=1)
-        .astype(jnp.bfloat16)
-        .reshape(row_count, 3 * head_cols)
-    )
-    grad_qkv = outer_sum(tokens_in, d_proj_low).reshape(model_width, 3, head_cols)
-    d_entry_part = jnp.einsum("tc,dc->td", d_proj_low, qkv_low, preferred_element_type=jnp.float32)
+    d_entry_part = jnp.einsum("tc,dc->td", d_proj[:row_count, :3 * head_cols], qkv_low, preferred_element_type=jnp.float32)
     input_grad = lax.psum(d_entry_part, "tensor") + spread(d_res_one)
     first_rank = (tensor_slot == 0).astype(jnp.float32)
     width_zero = jnp.zeros((model_width,), jnp.float32)
@@ -209,19 +502,19 @@
     def place_heads(partial_sum):
         return lax.dynamic_update_slice_in_dim(width_zero, partial_sum, tensor_slot * head_cols, 0)
 
-    grad_gains = jnp.stack([d_gain_one, d_gain_two]) * first_rank
+    grad_gains = vec[0:2] * first_rank
     grad_biases = jnp.stack(
         [
-            place_heads(jnp.sum(d_queries, axis=0)),
-            place_heads(jnp.sum(d_values, axis=0)),
-            jnp.sum(d_res_one, axis=0) * first_rank,
-            d_shift_one * first_rank,
-            jnp.sum(d_res_two, axis=0) * first_rank,
-            d_shift_two * first_rank,
+            place_heads(vec[2, :head_cols]),
+            place_heads(vec[2, head_cols:2 * head_cols]),
+            vec[3] * first_rank,
+            vec[4] * first_rank,
+            vec[5] * first_rank,
+            vec[6] * first_rank,
         ]
     )
     grad_bias_in = lax.dynamic_update_slice_in_dim(
-        jnp.zeros(bias_in.shape, jnp.float32), jnp.sum(d_pre, axis=0), tensor_slot * hidden_cols, 0
+        jnp.zeros(bias_in.shape, jnp.float32), vec[8], tensor_slot * hidden_cols, 0
     )
     grad_gains, grad_biases, grad_bias_in = lax.psum(
         (grad_gains, grad_biases, grad_bias_in), ("dp", "tensor")
@@ -230,7 +523,7 @@
     shard_rows = model_width // lax.axis_size("dp")
     owned = tuple(
         lax.psum_scatter(part, "dp", scatter_dimension=0, tiled=True)
-        for part in (grad_qkv, grad_out_proj, grad_in, grad_back)
+        for part in (grad_qkv, grad_out_proj, 0.5 * grad_in, 0.5 * grad_back)
     )
     clock = step[0].astype(jnp.float32)
     warm = warmup[0].astype(jnp.float32)

time: 903 us -> 599 us (0.66)
  waiting for transfers between devices: 611 us -> 275 us
  Pallas kernels: 0 us -> 87 us
  matrix products: 86.9 us -> 43.4 us
  local copies, waits for them, and re-layouts: 48.5 us -> 39.1 us
    psum x2 -> x0, waiting for transfers between devices: 94.6 us -> none  [the longest x1 60.6 us: on_device(): input_grad = lax.psum(d_entry_part, 'tensor') + spread(d_res_one)]
    pallas_call x0 -> x1, Pallas kernels: none -> 87 us  [k1_call(): pl.pallas_call(k1_kernel, out_shape=out_shape, in_specs=[sm, vm, vm, vm,...]
    psum x1, waiting for transfers between devices: 94.2 us -> 11.2 us  [on_device(): attn_sum = lax.psum(attn_part, 'tensor')]
    psum x1, waiting for transfers between devices: 78 us -> 0.01 us  [on_device(): down_sum = lax.psum(down_part, 'tensor')]
    reduce_scatter x4 -> x3, waiting for transfers between devices: 194 us -> 122 us  [on_device(): lax.psum_scatter(part, 'dp', scatter_dimension=0, tiled=True)]
    dot_general x19 -> x1, matrix products: 44.6 us -> 6.05 us  [on_device(): jnp.einsum('tc,dc->td', d_proj[:row_count, :3 * head_cols], qkv_low, pref...]
    unnamed x11 -> x10, waiting for transfers between devices: 0.18 us -> 32.7 us
    all_gather x1, waiting for transfers between devices: 46 us -> 22.7 us  [on_device(): lax.all_gather(change_rows[0], 'dp', axis=0, tiled=True)]
  transfers between devices with their start and end apart: 11 -> 9, of which waited for: 11 -> 8; matrix products, arithmetic and copies ran while one was open for 8% -> 17% of each run, Pallas kernels for 0% -> 15%
where the time goes in v2:
time: 599 us; the launch traced here: 591 us
  waiting for transfers between devices  275 us (46%)
  Pallas kernels  87 us (15%)
  blocking collectives  75.6 us (13%)
  other arithmetic  51.1 us (9%)
  matrix products  43.4 us (7%)
  local copies, waits for them, and re-layouts  39.1 us (7%)
  between operations  18.6 us (3%)
    reduce_scatter x3, waiting for transfers between devices, on_device(): lax.psum_scatter(part, 'dp', scatter_dimension=0, tiled=True)  122 us
    pallas_call x1, Pallas kernels, k1_call(): pl.pallas_call(k1_kernel, out_shape=out_shape, in_specs=[sm, vm, vm, vm,...  87 us
    all_gather x1, waiting for transfers between devices, on_device(): lax.all_gather(change_rows[3], 'dp', axis=0, tiled=True)  52.4 us
    psum x1, blocking collectives, on_device(): lax.psum((grad_gains, grad_biases, grad_bias_in), ('dp', 'tensor'))  42.5 us
    all_gather x1, waiting for transfers between devices, on_device(): lax.all_gather(change_rows[2], 'dp', axis=0, tiled=True)  34.5 us
    all_gather x1, blocking collectives, on_device(): lax.all_gather(change_rows[1], 'dp', axis=0, tiled=True)  33.1 us
    unnamed x10, waiting for transfers between devices  32.7 us
    all_gather x1, waiting for transfers between devices, on_device(): lax.all_gather(change_rows[0], 'dp', axis=0, tiled=True)  22.7 us
  transfers between devices with their start and end apart: 9, of which 8 were waited for; matrix products, arithmetic and copies ran while one was open for 17% of the time, Pallas kernels for 15%

profile of v2, /device:TPU:0, one launch (start us, length us, event | category | flops | bytes accessed | tf_op | source)
XLA Modules:
  0.0 591.0 jit_solution(1181166640557775562)
XLA Ops:
  8.1 1.6 convert_element_type.72
  9.6 3.6 fusion.15
  13.3 1.2 fusion.102
  14.5 1.2 slice_reduce_fusion.1
  16.2 1.9 squeeze.7
  18.1 1.4 fusion.65
  19.5 1.3 add.251
  20.8 1.1 multiply_convert_fusion
  21.9 1.7 add_reduce_fusion
  23.6 1.8 exponential_reduce_fusion
  25.4 1.8 copy-done
  27.2 0.9 squeeze.6
  28.6 5.5 fusion.27
  34.8 3.0 fusion.43
  38.0 87.0 %shard_map.324 = (f32[768,768]{1,0:T(8,128)}, f32[768,768]{1,0:T(8,128)}, f32[768,768]{1,0:T(8,128)}, bf16[1776,768]{1,0:T(8,128)(2,1)}, bf16[1536,192]{1,0:T(8,...) custom-call(s32[3]{0:T(128)} %lens.1, ...), custom_call_target="tpu_custom_call" | custom-call | tf_op jit(solution)/shard_map/pallas_call | solution.py:338
  125.0 2.9 slice.122
  128.0 3.4 broadcast_multiply_fusion.1
  131.5 1.6 broadcast_multiply_fusion
  133.4 2.3 slice.125
  138.3 1.4 dynamic_slice.23
  140.3 6.0 %fusion.21 = f32[1536,768]{1,0:T(8,128)} fusion(bf16[768,576]{0,1:T(8,128)(2,1)} %bitcast.153, bf16[1776,768]{1,0:T(8,128)(2,1)} %get-tuple-element.22), kind=kOutput, calls=%fused_computation.39 | convolution fusion | flops 1358954496 | bytes 7569408 | tf_op jit(solution)/shard_map/tc,dc->td/dot_general | solution.py:497
  146.3 11.2 %all-reduce.5.cloned.1.call-done = f32[1536,768]{1,0:T(8,128)} async-done(((f32[1536,768]{1,0:T(8,128)}), f32[1536,768]{1,0:T(8,128)}) %all-reduce.5.cloned.1.call-update) | async-done | bytes 4718608 | tf_op jit(solution)/shard_map/psum | solution.py:442
  157.5 3.2 fusion.99
  161.3 1.2 multiply_reduce_fusion.1
  163.1 32.5 %reduce-scatter.13.cloned.1.call-done = f32[96,576]{1,0:T(8,128)} async-done(((f32[768,576]{1,0:T(8,128)}), f32[96,576]{1,0:T(8,128)}) %reduce-scatter.13.cloned.1.call-update) | async-done | bytes 221200
  195.6 1.1 copy.83
  196.7 2.1 fusion.48
  198.8 1.9 copy.71
  200.8 19.3 %fusion.24 = f32[1536,768]{1,0:T(8,128)} fusion(f32[768]{0:T(1024)} %dynamic_slice.23, f32[768]{0:T(1024)} %get-tuple-element.78, f32[768]{0:T(1024)} %get-tuple-element.81, f32[1536]{0:T(1024)} %add_rsqrt_fusion.1, f32[1536]{0:T(1024)S(1)} %broadcast_multiply_fusion.3, f32[768,768]{1,0:T(8,128)} %wback_h.1, f32[768,768]{1,0:T(8,128)} %win_h.1, ...), kind=kOutput, calls=%fused_computation.41 | convolution fusion | flops 3712352256 | bytes 16539648 | tf_op jit(solution)/shard_map/tf,df->td/dot_general | solution.py:448
  220.1 48.0 %reduce-scatter.9.cloned.1.call-done = f32[96,768]{1,0:T(8,128)} async-done(((f32[768,768]{1,0:T(8,128)}), f32[96,768]{1,0:T(8,128)}) %reduce-scatter.9.cloned.1.call-update) | async-done | bytes 294928 | tf_op jit(solution)/shard_map/reduce_scatter | solution.py:525
  268.1 2.3 fusion.49
  271.1 0.8 fusion.104
  272.2 0.9 slice_reduce_fusion
  273.5 0.7 slice_multiply_fusion.2
  274.3 42.5 %all-reduce = (f32[2,768]{1,0:T(2,128)}, f32[6,768]{1,0:T(8,128)S(1)}, f32[3072]{0:T(1024)}) all-reduce(f32[2,768]{1,0:T(2,128)S(1)} %slice_multiply_fusion.2, f32[6,768]{1,0:T(8,128)S(1)} %stack.72, f32[3072]{0:T(1024)S(1)} %dynamic_update_slice.13), channel_id=1, replica_groups=mesh['dp'=8,'tensor'=4] {'dp','tensor'}, use_global_device_ids=true, to_apply=%region_13.14 | all-reduce | flops 9216 | bytes 73728 | tf_op jit(solution)/shard_map/psum | solution.py:519
  316.7 0.9 fusion.105
  318.3 1.0 constant_dynamic-slice_fusion
  319.3 0.8 select_compare_fusion
  320.2 1.4 fusion.97
  321.6 0.8 slice_multiply_fusion.1
  322.5 1.4 add_multiply_fusion.5
  324.5 4.2 fusion.38
  328.7 12.4 %reduce-scatter.11.cloned.1.call-done = f32[96,768]{1,0:T(8,128)} async-done(((f32[768,768]{1,0:T(8,128)}), f32[96,768]{1,0:T(8,128)}) %reduce-scatter.11.cloned.1.call-update) | async-done | bytes 294928 | tf_op jit(solution)/shard_map/reduce_scatter | solution.py:525
  341.1 2.2 fusion.50
  343.4 1.3 pad_maximum_fusion.6
  345.4 61.7 %reduce-scatter.7.cloned.1.call-done = f32[96,192]{1,0:T(8,128)} async-done(((f32[768,192]{1,0:T(8,128)}), f32[96,192]{1,0:T(8,128)}) %reduce-scatter.7.cloned.1.call-update) | async-done | bytes 73744 | tf_op jit(solution)/shard_map/reduce_scatter | solution.py:525
  407.1 1.7 fusion.54
  408.8 33.1 %all_gather.13 = f32[768,192]{1,0:T(8,128)S(1)} all-gather(f32[96,192]{1,0:T(8,128)S(1)} %get-tuple-element.107), channel_id=1, replica_groups=mesh['dp'=8,'tensor'=4] {'dp'}, dimensions={0}, use_global_device_ids=true | all-gather | bytes 663552 | tf_op jit(solution)/shard_map/all_gather | solution.py:547
  442.0 1.1 copy.76
  443.0 1.6 pad_maximum_fusion.3
  444.7 1.0 pad_maximum_fusion
  445.7 1.1 copy.77
  446.8 1.9 pad_maximum_fusion.1
  448.7 1.9 pad_maximum_fusion.2
  450.6 22.7 %all-gather.4.cloned.1.call-done = f32[768,3,192]{2,1,0:T(4,128)} async-done(((f32[96,3,192]{2,1,0:T(4,128)}), f32[768,3,192]{2,1,0:T(4,128)}) %all-gather.4.cloned.1.call-update) | async-done | bytes 1769488 | tf_op jit(solution)/shard_map/all_gather | solution.py:546
  473.2 4.2 copy.75
  477.5 5.0 fusion.101
  483.2 2.1 add_convert_fusion
  485.2 1.1 copy-done.3
  486.3 5.2 bitcast_add_fusion
  491.5 34.5 %all-gather.6.cloned.1.call-done = f32[768,768]{1,0:T(8,128)} async-done(((f32[96,768]{1,0:T(8,128)}), f32[768,768]{1,0:T(8,128)}) %all-gather.6.cloned.1.call-update) | async-done | bytes 2359312 | tf_op jit(solution)/shard_map/all_gather | solution.py:548
  525.9 52.4 %all-gather.8.cloned.1.call-done = f32[768,768]{1,0:T(8,128)} async-done(((f32[96,768]{1,0:T(8,128)}), f32[768,768]{1,0:T(8,128)}) %all-gather.8.cloned.1.call-update) | async-done | bytes 2359312 | tf_op jit(solution)/shard_map/all_gather | solution.py:549
  578.3 3.4 copy.129
  581.7 1.4 copy.130
  (90 shorter events, 8.9 us)
Async XLA Ops:
  8.0 149.4 %all-reduce.5.cloned.1.call-start = ((), (), s32[]{:S(2)}) async-start(), calls=%async_computation.4 | async-start | bytes 9437184 | tf_op jit(solution)/shard_map/psum | solution.py:442
  9.6 3.6 copy-start.7
  13.2 1.3 copy-start.10
  13.2 2.4 copy-start.19
  23.6 3.6 copy-start
  23.6 4.5 copy-start.20
  28.6 6.2 %copy-start.4 = (f32[768,192]{0,1:T(8,128)S(1)}, f32[768,192]{0,1:T(8,128)}, u32[]{:S(2)}) copy-start(f32[768,192]{0,1:T(8,128)} %param.29) | copy-start | bytes 1769476
  37.8 157.8 %reduce-scatter.13.cloned.1.call-start = ((), (), s32[]{:S(2)}) async-start(), calls=%async_computation.11 | async-start | bytes 2211840
  127.9 3.5 copy-start.6
  128.0 140.2 %reduce-scatter.9.cloned.1.call-start = ((), (), s32[]{:S(2)}) async-start(), calls=%async_computation.7 | async-start | bytes 2654208 | tf_op jit(solution)/shard_map/reduce_scatter | solution.py:525
  131.4 209.7 %reduce-scatter.11.cloned.1.call-start = ((), (), s32[]{:S(2)}) async-start(), calls=%async_computation.9 | async-start | bytes 2654208 | tf_op jit(solution)/shard_map/reduce_scatter | solution.py:525
  131.5 4.2 copy-start.12
  131.5 8.2 %copy-start.9 = (f32[2,96,3,192]{3,1,2,0:T(8,128)S(1)}, f32[2,96,3,192]{3,1,2,0:T(8,128)}, u32[]{:S(2)}) copy-start(f32[2,96,3,192]{3,1,2,0:T(8,128)} %param.35) | copy-start | bytes 1327108
  133.1 274.0 %reduce-scatter.7.cloned.1.call-start = ((), (), s32[]{:S(2)}) async-start(), calls=%async_computation.6 | async-start | bytes 884736 | tf_op jit(solution)/shard_map/reduce_scatter | solution.py:525
  135.7 337.6 %all-gather.4.cloned.1.call-start = ((), (), s32[]{:S(2)}) async-start(), calls=%async_computation.5 | async-start | bytes 3538944 | tf_op jit(solution)/shard_map/all_gather | solution.py:546
  140.2 17.2 %copy-start.2 = (bf16[1536,768]{1,0:T(8,128)(2,1)S(1)}, bf16[1536,768]{1,0:T(8,128)(2,1)}, u32[]{:S(2)}) copy-start(bf16[1536,768]{1,0:T(8,128)(2,1)} %x_h.1) | copy-start | bytes 7077892
  157.5 3.9 copy-start.1
  200.7 276.7 %all-reduce.7.cloned.1.call-start = ((), (), s32[]{:S(2)}) async-start(), calls=%async_computation.12 | async-start | bytes 18874368 | tf_op jit(solution)/shard_map/psum | solution.py:449
  220.0 50.4 %copy-start.14 = (s32[1536]{0:T(1024)S(1)}, s32[1536]{0:T(1024)}, u32[]{:S(2)}) copy-start(s32[1536]{0:T(1024)} %param.23) | copy-start | bytes 18436
  220.0 97.6 %copy-start.11 = (f32[6,768]{1,0:T(8,128)S(1)}, f32[6,768]{1,0:T(8,128)}, u32[]{:S(2)}) copy-start(f32[6,768]{1,0:T(8,128)} %biases.1) | copy-start | bytes 55300
  220.1 104.4 %copy-start.8 = (f32[240,768]{1,0:T(8,128)S(1)}, f32[240,768]{1,0:T(8,128)}, u32[]{:S(2)}) copy-start(f32[240,768]{1,0:T(8,128)} %get-tuple-element.23) | copy-start | bytes 2211844
  220.1 305.8 %all-gather.6.cloned.1.call-start = ((), (), s32[]{:S(2)}) async-start(), calls=%async_computation.8 | async-start | bytes 2654208 | tf_op jit(solution)/shard_map/all_gather | solution.py:548
  270.4 307.9 %all-gather.8.cloned.1.call-start = ((), (), s32[]{:S(2)}) async-start(), calls=%async_computation.10 | async-start | bytes 2654208 | tf_op jit(solution)/shard_map/all_gather | solution.py:549
  444.7 32.8 %copy-start.13 = (f32[1536]{0:T(1024)S(1)}, f32[1536]{0:T(1024)}, u32[]{:S(2)}) copy-start(f32[1536]{0:T(1024)} %add_rsqrt_fusion.1) | copy-start | bytes 18436
  444.7 32.8 %copy-start.15 = (f32[768]{0:T(1024)S(1)}, f32[768]{0:T(1024)}, u32[]{:S(2)}) copy-start(f32[768]{0:T(1024)} %get-tuple-element.77) | copy-start | bytes 9220
  444.7 32.8 %copy-start.16 = (f32[768]{0:T(1024)S(1)}, f32[768]{0:T(1024)}, u32[]{:S(2)}) copy-start(f32[768]{0:T(1024)} %get-tuple-element.78) | copy-start | bytes 9220
  444.7 32.8 %copy-start.18 = (f32[768]{0:T(1024)S(1)}, f32[768]{0:T(1024)}, u32[]{:S(2)}) copy-start(f32[768]{0:T(1024)} %get-tuple-element.81) | copy-start | bytes 9220
  482.5 0.7 copy-start.17
  483.1 3.2 copy-start.3
  578.3 3.4 copy-start.5
Sparse Core Ops, SparseCore 0:
  37.9 119.4 all-reduce.4
  220.2 170.4 all-reduce.6
Sparse Core Ops, SparseCore 1:
  128.1 67.5 reduce-scatter.12
  199.9 68.1 reduce-scatter.8
  272.5 68.6 reduce-scatter.10
  345.4 61.7 reduce-scatter.6
  409.9 63.3 all-gather.3
  475.5 50.4 all-gather.5
  528.0 50.3 all-gather.7
